TPU v7x, 32 devices: a whole 2x2x4 slice. The times are simulated.
32 devices in a mesh: dom: 32 (over z, y, x, core).
Axes of the slice: x: 2, y: 2, z: 4, core: 2. Of those that a mesh axis runs over, the one named last changes fastest.
Arguments:
- solution: float32 [4, 20, 65536], P(None, None, 'dom'), may hold values from -6 to 6
- register: float32 [4, 20, 65536], P(None, None, 'dom'), may hold values from -4 to 4
- geometry: float32 [9, 65536], P(None, 'dom'), may hold values from -4 to 4
- normals: float32 [3, 4, 65536], P(None, None, 'dom'), may hold values from -1 to 1, as said below
- face_scale: float32 [4, 65536], P(None, 'dom'), may hold values from 0.5 to 2
- impedance: float32 [16], replicated, may hold values from 0.2 to 5
- neighbour: int32 [4, 65536], P(None, 'dom'), may hold values from -1 to 9215
- orientation: int32 [4, 65536], P(None, 'dom'), may hold values from 0 to 2
- wall_material: int32 [4, 65536], P(None, 'dom'), may hold values from 0 to 15
- send_faces: int32 [256, 128], P('dom'), may hold values from -1 to 8191, as said below
Outputs:
- solution_next: float32 [4, 20, 65536], P(None, None, 'dom')
- register_next: float32 [4, 20, 65536], P(None, None, 'dom')
- absorbed: float32 [2, 16], replicated
Inputs may be any that keep to these rules, and one draw needn't show every extreme that they name: `send_faces`: row j of partition d lists distinct local faces (numbered f * 2048 + e) sent to partition d + o_j in slot order, then -1; rows for partitions outside the mesh are all -1; the lists of two partitions for each other have equal lengths, and at most 128 faces go from one partition to another, a bound that is reached. Each face's three entries form a unit vector, and two faces that name each other as neighbours have opposite normals.
All inputs are finite; a program needn't handle non-finite values.
Results may differ from a plain program's by a relative error of at most 0.0003.
Values sent between devices are 32-bit elements; how exact they have to be, the bound alone decides.
A program may use at most 128 MiB of HBM per device.

v0:
```python
import math

import jax
import jax.numpy as jnp
from jax import lax
from jax.sharding import PartitionSpec as P

NMAT = 16


section_decay = (-567301805773.0 / 1357537059087.0, -2404267990393.0 / 2016746695238.0)
section_weight = (1720146321549.0 / 2090206949498.0, 3134564353537.0 / 4481467310338.0)
time_step = 0.002


def mat_product(left, right):
    inner = len(right)
    return [
        [sum((left[i][k] * right[k][j] for k in range(inner))) for j in range(len(right[0]))]
        for i in range(len(left))
    ]


def flipped(matrix):
    return [list(row) for row in zip(*matrix)]


def solve_rows(matrix, right):
    size = len(matrix)
    augmented = [list(matrix[i]) + list(right[i]) for i in range(size)]
    for column in range(size):
        pivot = max(range(column, size), key=lambda r: abs(augmented[r][column]))
        augmented[column], augmented[pivot] = (augmented[pivot], augmented[column])
        leader = augmented[column][column]
        augmented[column] = [value / leader for value in augmented[column]]
        for other in range(size):
            if other != column:
                factor = augmented[other][column]
                if factor != 0.0:
                    augmented[other] = [
                        a - factor * b for a, b in zip(augmented[other], augmented[column])
                    ]
    return [row[size:] for row in augmented]


def identity_rows(size):
    return [[1.0 if i == j else 0.0 for j in range(size)] for i in range(size)]


def dg_tables():
    lattice = [(i, j, k) for i in range(4) for j in range(4 - i) for k in range(4 - i - j)]
    coords = [(i / 3.0, j / 3.0, k / 3.0) for i, j, k in lattice]
    vander = [[x**a * y**b * z**c for a, b, c in lattice] for x, y, z in coords]
    inverse = solve_rows(vander, identity_rows(20))
    gradient_rows = []
    for d in range(3):
        derived = []
        for point in coords:
            row = []
            for powers in lattice:
                if powers[d] == 0:
                    row.append(0.0)
                else:
                    lowered = [powers[0], powers[1], powers[2]]
                    lowered[d] = lowered[d] - 1
                    row.append(
                        powers[d]
                        * point[0] ** lowered[0]
                        * point[1] ** lowered[1]
                        * point[2] ** lowered[2]
                    )
            derived.append(row)
        gradient_rows.extend(mat_product(derived, inverse))
    mono_mass = [
        [
            math.factorial(a + p)
            * math.factorial(b + q)
            * math.factorial(c + r)
            / math.factorial(a + b + c + p + q + r + 3)
            for p, q, r in lattice
        ]
        for a, b, c in lattice
    ]
    mass_matrix = mat_product(mat_product(flipped(inverse), mono_mass), inverse)
    plane_points = [(a, b) for a in range(4) for b in range(4 - a)]
    face_coords = [(a / 3.0, b / 3.0) for a, b in plane_points]
    vander_face = [[x**a * y**b for a, b in plane_points] for x, y in face_coords]
    inverse_face = solve_rows(vander_face, identity_rows(10))
    mono_face = [
        [
            math.factorial(a + p) * math.factorial(b + q) / math.factorial(a + b + p + q + 2)
            for p, q in plane_points
        ]
        for a, b in plane_points
    ]
    face_mass = mat_product(mat_product(flipped(inverse_face), mono_face), inverse_face)
    position = {point: n for n, point in enumerate(lattice)}
    builders = [
        lambda a, b: (a, b, 0),
        lambda a, b: (a, 0, b),
        lambda a, b: (0, a, b),
        lambda a, b: (a, b, 3 - a - b),
    ]
    face_nodes = [[position[builder(a, b)] for a, b in plane_points] for builder in builders]
    surface = [[0.0] * 40 for n in range(20)]
    for f in range(4):
        for n in range(10):
            for m in range(10):
                surface[face_nodes[f][n]][f * 10 + m] = face_mass[n][m]
    lift_matrix = solve_rows(mass_matrix, surface)
    rotations = []
    for t in range(3):
        mapping = []
        for a, b in plane_points:
            triple = (b, a, 3 - a - b)
            for s in range(t):
                triple = (triple[1], triple[2], triple[0])
            mapping.append(plane_points.index((triple[0], triple[1])))
        rotations.append(mapping)
    return (gradient_rows, lift_matrix, face_nodes, rotations)


def peer_offsets(half_span):
    return [j - half_span if j < half_span else j - half_span + 1 for j in range(2 * half_span)]


def node_major_traces(solution, node_order):
    elem_count = solution.shape[2]
    return solution[:, node_order, :].reshape(4, 10, 4 * elem_count)


def orient_values(values, orientation, rotate_tables):
    turned = jnp.einsum("tnk,fkx->tfnx", rotate_tables, values, precision=lax.Precision.HIGHEST)
    return jnp.where(orientation == 0, turned[0], jnp.where(orientation == 1, turned[1], turned[2]))


def wall_reflection(materials, impedance):
    material_ids = jnp.arange(impedance.shape[0], dtype=jnp.int32)
    picked = jnp.sum(
        jnp.where(
            materials[None, :] == material_ids[:, None], impedance[:, None], jnp.float32(0.0)
        ),
        axis=0,
    )
    return (picked - 1.0) / (picked + 1.0)


def face_flux(inner_trace, outer_trace, wall_mask, normal_flat, scale_flat, reflect):
    press_in = inner_trace[0]
    press_out = outer_trace[0]
    normal_in = (
        normal_flat[0] * inner_trace[1]
        + normal_flat[1] * inner_trace[2]
        + normal_flat[2] * inner_trace[3]
    )
    normal_out = (
        normal_flat[0] * outer_trace[1]
        + normal_flat[1] * outer_trace[2]
        + normal_flat[2] * outer_trace[3]
    )
    jump_press = jnp.where(wall_mask, (1.0 - reflect) * press_in, press_in - press_out)
    jump_normal = jnp.where(wall_mask, (1.0 + reflect) * normal_in, normal_in - normal_out)
    flux_press = 0.5 * scale_flat * (jump_normal - jump_press)
    flux_stack = jnp.stack(
        [
            flux_press,
            -normal_flat[0] * flux_press,
            -normal_flat[1] * flux_press,
            -normal_flat[2] * flux_press,
        ]
    )
    incoming = press_in + normal_in
    wall_loss = 0.25 * scale_flat * (1.0 - reflect * reflect) * incoming * incoming
    return (flux_stack, wall_loss)


def material_sums(wall_loss, wall_mask, materials, material_count):
    per_face = jnp.where(wall_mask, jnp.sum(wall_loss, axis=0), jnp.float32(0.0))
    material_ids = jnp.arange(material_count, dtype=jnp.int32)
    return jnp.sum(
        jnp.where(materials[None, :] == material_ids[:, None], per_face[None, :], jnp.float32(0.0)),
        axis=1,
    )


def assemble(solution, geometry, flux_stack, gradient_ops, lift_node_major):
    elem_count = solution.shape[2]
    gradients = jnp.einsum(
        "km,fme->fke", gradient_ops, solution, precision=lax.Precision.HIGHEST
    ).reshape(4, 3, 20, elem_count)
    metric = geometry.reshape(3, 3, elem_count)

    def physical_derivative(field_index, i):
        return (
            metric[i, 0] * gradients[field_index, 0]
            + metric[i, 1] * gradients[field_index, 1]
            + metric[i, 2] * gradients[field_index, 2]
        )

    flux_faces = flux_stack.reshape(4, 40, elem_count)
    lifted = jnp.einsum("nk,fke->fne", lift_node_major, flux_faces, precision=lax.Precision.HIGHEST)
    divergence = physical_derivative(1, 0) + physical_derivative(2, 1) + physical_derivative(3, 2)
    return jnp.stack(
        [
            lifted[0] - divergence,
            lifted[1] - physical_derivative(0, 0),
            lifted[2] - physical_derivative(0, 1),
            lifted[3] - physical_derivative(0, 2),
        ]
    )


def local(
    solution,
    register,
    geometry,
    normals,
    face_scale,
    impedance,
    neighbour,
    orientation,
    wall_material,
    send_faces,
):
    grad_rows, lift_rows, face_nodes, rotations = dg_tables()
    gradient_ops = jnp.asarray(grad_rows, dtype=jnp.float32)
    lift_reordered = [[row[f * 10 + m] for m in range(10) for f in range(4)] for row in lift_rows]
    lift_node_major = jnp.asarray(lift_reordered, dtype=jnp.float32)
    node_order = jnp.array([face_nodes[f][m] for m in range(10) for f in range(4)], dtype=jnp.int32)
    rotate_tables = jnp.asarray(
        [
            [[1.0 if rotations[t][n] == k else 0.0 for k in range(10)] for n in range(10)]
            for t in range(3)
        ],
        dtype=jnp.float32,
    )
    elem_count = solution.shape[2]
    face_count = 4 * elem_count
    blocks = send_faces.shape[0]
    capacity = send_faces.shape[1]
    offsets = peer_offsets(blocks // 2)
    devices = lax.axis_size("dom")
    my_index = lax.axis_index("dom")
    link_codes = neighbour.reshape(face_count)
    orient_flat = orientation.reshape(face_count)
    materials = wall_material.reshape(face_count)
    wall_mask = link_codes < 0
    reflect = wall_reflection(materials, impedance)
    normal_flat = normals.reshape(3, face_count)
    scale_flat = face_scale.reshape(face_count)
    gather_index = jnp.maximum(link_codes, 0)
    send_index = jnp.maximum(send_faces, 0)
    send_live = send_faces >= 0
    peer_index = my_index + jnp.array(offsets, dtype=jnp.int32)
    peer_valid = (peer_index >= 0) & (peer_index < devices)
    norm_factor = NMAT / (devices * elem_count)
    absorbed = []
    for section_index in range(2):
        inner_trace = node_major_traces(solution, node_order)
        flat_inner = inner_trace.reshape(40, face_count)
        outgoing = jnp.where(
            send_live[None], jnp.take(flat_inner, send_index, axis=1), jnp.float32(0.0)
        )
        target = jnp.where(peer_valid, peer_index, devices)
        buffer = (
            jnp.zeros((40, devices, capacity), jnp.float32).at[:, target].set(outgoing, mode="drop")
        )
        arrived = lax.all_to_all(buffer, "dom", split_axis=1, concat_axis=1, tiled=True)
        incoming = jnp.take(arrived, jnp.clip(peer_index, 0, devices - 1), axis=1)
        trace_table = jnp.concatenate([flat_inner, incoming.reshape(40, blocks * capacity)], axis=1)
        outer_trace = jnp.take(trace_table, gather_index, axis=1).reshape(4, 10, face_count)
        outer_trace = orient_values(outer_trace, orient_flat, rotate_tables)
        flux_stack, wall_loss = face_flux(
            inner_trace, outer_trace, wall_mask, normal_flat, scale_flat, reflect
        )
        rhs_local = assemble(solution, geometry, flux_stack, gradient_ops, lift_node_major)
        totals = material_sums(wall_loss, wall_mask, materials, impedance.shape[0])
        absorbed.append(lax.psum(totals, "dom") * norm_factor)
        register = section_decay[section_index] * register + time_step * rhs_local
        solution = solution + section_weight[section_index] * register
    absorbed_out = jnp.stack(absorbed)
    return (solution, register, absorbed_out)


def solution(mesh):
    in_specs = (
        P(None, None, "dom"),
        P(None, None, "dom"),
        P(None, "dom"),
        P(None, None, "dom"),
        P(None, "dom"),
        P(),
        P(None, "dom"),
        P(None, "dom"),
        P(None, "dom"),
        P("dom", None),
    )
    out_specs = (P(None, None, "dom"), P(None, None, "dom"), P())
    return jax.shard_map(local, mesh=mesh, in_specs=in_specs, out_specs=out_specs, check_vma=False)
```

profile of v0, /device:TPU:0, one launch (start us, length us, event | category | flops | bytes accessed | tf_op | source)
XLA Modules:
  0.0 276.5 jit_solution(9091995785568347228)
XLA Ops:
  2.7 2.4 gather_fusion
  5.1 1.8 copy.174
  6.9 1.9 reshape_reshape.6
  8.8 2.7 copy.175
  11.6 5.0 %gather_fusion.2 = f32[1024,40]{1,0:T(8,128)S(1)} fusion(f32[40,8192]{0,1:T(8,128)} %copy.175, s32[1024]{0:T(1024)S(1)} %bitcast_clamp_fusion), kind=kCustom, calls=%fused_computation.clone | custom fusion | bytes 331776 | tf_op jit(solution)/shard_map/jit(_take)/gather | solution.py:262
  17.7 2.2 scatter_fusion
  19.9 7.8 %all-to-all-start = ((f32[40,32,128]{2,0,1:T(8,128)}), f32[40,32,128]{2,0,1:T(8,128)}, u32[]{:S(2)}, u32[]{:S(2)}) async-start(f32[40,32,128]{2,0,1:T(8,128)} %scatter_fusion), calls=%async_computation | async-start | bytes 1310720 | tf_op jit(solution)/shard_map/all_to_all | solution.py:268
  29.6 3.7 %slice_reduce_fusion.7 = (f32[40,2048]{1,0:T(8,128)S(1)}, f32[40,2048]{1,0:T(8,128)}, f32[40,2048]{1,0:T(8,128)}, f32[40,2048]{1,0:T(8,128)S(1)}) fusion(f32[4,40,2048]{2,0,1:T(4,128)S(1)} %bitcast.388), kind=kLoop, calls=%fused_computation.90 | loop fusion | bytes 2621440 | tf_op jit(solution)/shard_map/slice | solution.py:152
  37.1 1.0 squeeze.165
  45.4 2.1 convolution_bitcast_fusion.3
  47.5 2.5 copy.183
  51.5 6.5 %fusion.111 = (f32[1,1,20,2048]{3,0,2,1:T(1,128)}, f32[1,1,20,2048]{3,0,2,1:T(1,128)}, f32[1,1,20,2048]{3,0,2,1:T(1,128)}, f32[1,1,20,2048]{3,0,2,1:T(1,128)}, f...) fusion(f32[4,3,20,2048]{3,0,2,1:T(4,128)} %bitcast.391), kind=kLoop, calls=%fused_computation.235 | loop fusion | bytes 3932160 | tf_op jit(solution)/shard_map/slice | solution.py:195
  58.0 1.6 gather_fusion.3
  59.8 1.2 pad_maximum_fusion
  61.0 4.0 %copy.178 = f32[40,9216]{0,1:T(8,128)} copy(f32[40,9216]{1,0:T(8,128)} %pad_maximum_fusion) | data formatting | bytes 2949120 | tf_op jit(solution)/shard_map/concatenate | solution.py:270
  65.0 30.2 %gather_fusion.4 = f32[8192,40]{1,0:T(8,128)} fusion(f32[40,9216]{0,1:T(8,128)} %copy.178, s32[8192]{0:T(1024)S(1)} %copy-done.52), kind=kCustom, calls=%fused_computation.2.clone | custom fusion | bytes 2654208 | tf_op jit(solution)/shard_map/jit(_take)/gather | solution.py:271
  95.2 7.4 %select_bitcast_fusion.1 = f32[40,8192]{0,1:T(8,128)} fusion(f32[8192,40]{1,0:T(8,128)} %gather_fusion.4, pred[8192]{0:T(1024)(128)(4,1)S(1)} %copy-done.83), kind=kLoop, calls=%fused_computation.13 | loop fusion | flops 327680 | bytes 2629632 | tf_op jit(solution)/shard_map/jit(_take)/select_n | solution.py:271
  102.7 3.8 %copy.179 = f32[40,8192]{1,0:T(8,128)} copy(f32[40,8192]{0,1:T(8,128)} %select_bitcast_fusion.1) | data formatting | bytes 2621440 | tf_op jit(solution)/shard_map/jit(_take)/select_n | solution.py:271
  106.5 1.5 reshape.2610
  108.1 5.8 %convolution_bitcast_fusion.1 = f32[3,4,10,8192]{3,2,0,1:T(8,128)S(1)} fusion(f32[3,10,10,1]{2,1,0,3:T(8,128)S(1)} %copy-done.95, f32[4,10,8192,1]{2,1,0,3:T(8,128)S(1)} %reshape.2610), kind=kOutput, calls=%fused_computation.11 | convolution fusion | flops 117964800 | bytes 5244080 | tf_op jit(solution)/shard_map/tnk,fkx->tfnx/dot_general | solution.py:133
  115.5 1.1 broadcast_multiply_fusion.5
  119.5 2.1 convolution_bitcast_fusion.5
  124.1 1.5 gather_fusion.1
  125.6 4.5 %slice_reduce_fusion.3 = (f32[40,2048]{1,0:T(8,128)}, f32[40,2048]{1,0:T(8,128)}, f32[40,2048]{1,0:T(8,128)}, f32[40,2048]{1,0:T(8,128)}) fusion(f32[4,40,2048]{2,0,1:T(4,128)S(1)} %bitcast.389), kind=kLoop, calls=%fused_computation.86 | loop fusion | bytes 2621440 | tf_op jit(solution)/shard_map/slice | solution.py:152
  130.9 2.0 squeeze.206
  132.8 1.9 squeeze.207
  134.8 1.9 squeeze.208
  136.7 1.0 squeeze.209
  138.3 2.7 copy.199
  141.0 5.0 %gather_fusion.5 = f32[1024,40]{1,0:T(8,128)S(1)} fusion(f32[40,8192]{0,1:T(8,128)} %copy.199, s32[1024]{0:T(1024)S(1)} %copy-done.91), kind=kCustom, calls=%fused_computation.3.clone | custom fusion | bytes 331776 | tf_op jit(solution)/shard_map/jit(_take)/gather | solution.py:262
  147.2 2.2 scatter_fusion.1
  149.3 6.0 %all-to-all-start.1 = ((f32[40,32,128]{2,0,1:T(8,128)}), f32[40,32,128]{2,0,1:T(8,128)}, u32[]{:S(2)}, u32[]{:S(2)}) async-start(f32[40,32,128]{2,0,1:T(8,128)} %scatter_fusion.1), calls=%async_computation.1 | async-start | bytes 1310720 | tf_op jit(solution)/shard_map/all_to_all | solution.py:268
  155.4 2.7 fusion.22
  159.0 41.2 %all-reduce = (f32[16]{0:T(128)}, f32[16]{0:T(128)}) all-reduce(f32[16]{0:T(128)} %get-tuple-element.32, f32[16]{0:T(128)} %get-tuple-element.31), channel_id=1, replica_groups=mesh['dom'=32] {'dom'}, use_global_device_ids=true, to_apply=%region_8.12 | all-reduce | flops 32 | bytes 256 | tf_op jit(solution)/shard_map/psum | solution.py:278
  203.2 2.6 convolution_bitcast_fusion.2
  205.8 1.3 copy.205
  207.7 2.7 fusion.110
  210.5 1.8 gather_fusion.6
  212.3 1.2 pad_maximum_fusion.1
  213.6 4.0 %copy.202 = f32[40,9216]{0,1:T(8,128)} copy(f32[40,9216]{1,0:T(8,128)} %pad_maximum_fusion.1) | data formatting | bytes 2949120 | tf_op jit(solution)/shard_map/concatenate | solution.py:270
  217.6 30.2 %gather_fusion.7 = f32[8192,40]{1,0:T(8,128)} fusion(f32[40,9216]{0,1:T(8,128)} %copy.202, s32[8192]{0:T(1024)S(1)} %copy-done.53), kind=kCustom, calls=%fused_computation.5.clone | custom fusion | bytes 2654208 | tf_op jit(solution)/shard_map/jit(_take)/gather | solution.py:271
  247.8 7.4 %select_bitcast_fusion = f32[40,8192]{0,1:T(8,128)} fusion(f32[8192,40]{1,0:T(8,128)} %gather_fusion.7, pred[8192]{0:T(1024)(128)(4,1)S(1)} %copy-done.84), kind=kLoop, calls=%fused_computation.12 | loop fusion | flops 327680 | bytes 2629632 | tf_op jit(solution)/shard_map/jit(_take)/select_n | solution.py:271
  255.2 3.8 %copy.203 = f32[40,8192]{1,0:T(8,128)} copy(f32[40,8192]{0,1:T(8,128)} %select_bitcast_fusion) | data formatting | bytes 2621440 | tf_op jit(solution)/shard_map/jit(_take)/select_n | solution.py:271
  259.1 1.5 reshape.2614
  260.6 6.6 %convolution_bitcast_fusion = f32[3,4,10,8192]{3,2,1,0:T(8,128)S(1)} fusion(f32[4,10,8192,1]{2,1,0,3:T(8,128)S(1)} %reshape.2614, f32[3,10,10,1]{2,1,3,0:T(8,128)} %constant.101), kind=kOutput, calls=%fused_computation.10 | convolution fusion | flops 117964800 | bytes 5244080 | tf_op jit(solution)/shard_map/tnk,fkx->tfnx/dot_general | solution.py:133
  270.1 1.7 convolution_bitcast_fusion.4
  273.8 1.3 copy.218
  275.0 1.3 copy.219
  (299 shorter events, 35.5 us)
Async XLA Ops:
  1.3 10.2 %copy-start.90 = (s32[1024]{0:T(1024)}, s32[1024]{0:T(1024)S(1)}, u32[]{:S(2)}) copy-start(s32[1024]{0:T(1024)S(1)} %bitcast_clamp_fusion) | copy-start | bytes 12292
  2.0 14.8 %copy-start.96 = (pred[8,128]{1,0:T(8,128)(4,1)}, pred[8,128]{1,0:T(8,128)(4,1)S(1)}, u32[]{:S(2)}) copy-start(pred[8,128]{1,0:T(8,128)(4,1)S(1)} %get-tuple-element.98) | copy-start | bytes 3076
  2.0 14.8 %copy-start.98 = (pred[8,128]{1,0:T(8,128)(4,1)}, pred[8,128]{1,0:T(8,128)(4,1)S(1)}, u32[]{:S(2)}) copy-start(pred[8,128]{1,0:T(8,128)(4,1)S(1)} %get-tuple-element.99) | copy-start | bytes 3076
  2.7 4.3 %copy-start.101 = (s32[1024]{0:T(1024)}, s32[1024]{0:T(1024)S(1)}, u32[]{:S(2)}) copy-start(s32[1024]{0:T(1024)S(1)} %pad_clamp_fusion.1) | copy-start | bytes 12292
  11.6 5.2 %copy-start.107 = (s32[8]{0:T(128)S(1)}, s32[8]{0:T(128)}, u32[]{:S(2)}) copy-start(s32[8]{0:T(128)} %constant.40.clone) | copy-start | bytes 100
  16.6 11.7 %copy-start.81 = (s32[4,2048]{1,0:T(4,128)S(1)}, s32[4,2048]{1,0:T(4,128)}, u32[]{:S(2)}) copy-start(s32[4,2048]{1,0:T(4,128)} %param.27) | copy-start | bytes 98308
  16.8 12.2 %copy-start.104 = (s32[8]{0:T(128)}, s32[8]{0:T(128)S(1)}, u32[]{:S(2)}) copy-start(s32[8]{0:T(128)S(1)} %compare_select_fusion.2) | copy-start | bytes 100
  19.9 38.1 %all-to-all-start = ((f32[40,32,128]{2,0,1:T(8,128)}), f32[40,32,128]{2,0,1:T(8,128)}, u32[]{:S(2)}, u32[]{:S(2)}) async-start(f32[40,32,128]{2,0,1:T(8,128)} %scatter_fusion), calls=%async_computation | async-start | bytes 1310720 | tf_op jit(solution)/shard_map/all_to_all | solution.py:268
  33.3 3.9 %copy-start.7 = (f32[40,2048]{1,0:T(8,128)S(1)}, f32[40,2048]{1,0:T(8,128)}, u32[]{:S(2)}) copy-start(f32[40,2048]{1,0:T(8,128)} %get-tuple-element.27) | copy-start | bytes 983044
  34.2 4.9 %copy-start.6 = (f32[40,2048]{1,0:T(8,128)S(1)}, f32[40,2048]{1,0:T(8,128)}, u32[]{:S(2)}) copy-start(f32[40,2048]{1,0:T(8,128)} %get-tuple-element.26) | copy-start | bytes 983044
  36.2 4.8 %copy-start.93 = (s32[4,2048]{1,0:T(4,128)S(1)}, s32[4,2048]{1,0:T(4,128)}, u32[]{:S(2)}) copy-start(s32[4,2048]{1,0:T(4,128)} %param.28) | copy-start | bytes 98308
  36.2 6.0 %copy-start.82 = (f32[3,4,2048]{2,1,0:T(4,128)S(1)}, f32[3,4,2048]{2,1,0:T(4,128)}, u32[]{:S(2)}) copy-start(f32[3,4,2048]{2,1,0:T(4,128)} %param.24) | copy-start | bytes 294916
  37.1 5.7 %copy-start.92 = (f32[4,2048]{1,0:T(4,128)S(1)}, f32[4,2048]{1,0:T(4,128)}, u32[]{:S(2)}) copy-start(f32[4,2048]{1,0:T(4,128)} %param.25) | copy-start | bytes 98308
  37.1 5.8 %copy-start.94 = (s32[4,2048]{1,0:T(4,128)S(1)}, s32[4,2048]{1,0:T(4,128)}, u32[]{:S(2)}) copy-start(s32[4,2048]{1,0:T(4,128)} %param.29) | copy-start | bytes 98308
  37.1 8.2 %copy-start = (f32[4,20,2048]{2,0,1:T(4,128)S(1)}, f32[4,20,2048]{2,0,1:T(4,128)}, u32[]{:S(2)}) copy-start(f32[4,20,2048]{2,0,1:T(4,128)} %param.21) | copy-start | bytes 1966084
  37.1 8.2 %copy-start.89 = (f32[60,20,1]{0,1,2:T(8,128)S(1)}, f32[60,20,1]{0,1,2:T(8,128)}, u32[]{:S(2)}) copy-start(f32[60,20,1]{0,1,2:T(8,128)} %constant.100) | copy-start | bytes 14404
  42.9 7.1 %copy-start.61 = (s32[1,16,4,128]{3,1,2,0:T(8,128)}, s32[1,16,4,128]{3,1,2,0:T(8,128)S(1)}, u32[]{:S(2)}) copy-start(s32[1,16,4,128]{3,1,2,0:T(8,128)S(1)} %copy.253) | copy-start | bytes 98308
  47.4 2.6 copy-start.80
  47.5 2.6 copy-start.106
  50.3 7.8 %copy-start.100 = (s32[1024]{0:T(1024)}, s32[1024]{0:T(1024)S(1)}, u32[]{:S(2)}) copy-start(s32[1024]{0:T(1024)S(1)} %pad_clamp_fusion) | copy-start | bytes 12292
  50.9 63.5 %copy-start.50 = (f32[8192]{0:T(1024)}, f32[8192]{0:T(1024)S(1)}, u32[]{:S(2)}) copy-start(f32[8192]{0:T(1024)S(1)} %get-tuple-element.91) | copy-start | bytes 98308
  51.5 8.2 %copy-start.102 = (pred[8]{0:T(512)(128)(4,1)S(1)}, pred[8]{0:T(512)(128)(4,1)}, u32[]{:S(2)}) copy-start(pred[8]{0:T(512)(128)(4,1)} %get-tuple-element.41) | copy-start | bytes 28
  61.0 4.0 %copy-start.52 = (s32[8192]{0:T(1024)S(1)}, s32[8192]{0:T(1024)}, u32[]{:S(2)}) copy-start(s32[8192]{0:T(1024)} %fusion.104) | copy-start | bytes 98308
  65.0 30.2 %copy-start.83 = (pred[8192]{0:T(1024)(128)(4,1)S(1)}, pred[8192]{0:T(1024)(128)(4,1)}, u32[]{:S(2)}) copy-start(pred[8192]{0:T(1024)(128)(4,1)} %compare_and_fusion) | copy-start | bytes 24580
  108.1 5.9 %copy-start.85 = (pred[1,16,4,128]{3,1,2,0:T(8,128)(4,1)S(1)}, pred[1,16,4,128]{3,1,2,0:T(8,128)(4,1)}, u32[]{:S(2)}) copy-start(pred[1,16,4,128]{3,1,2,0:T(8,128)(4,1)} %copy.257) | copy-start | bytes 24580
  108.1 5.9 %copy-start.87 = (pred[1,16,4,128]{3,1,2,0:T(8,128)(4,1)S(1)}, pred[1,16,4,128]{3,1,2,0:T(8,128)(4,1)}, u32[]{:S(2)}) copy-start(pred[1,16,4,128]{3,1,2,0:T(8,128)(4,1)} %copy.259) | copy-start | bytes 24580
  116.6 2.7 copy-start.17
  119.5 2.6 copy-start.38
  119.5 2.6 copy-start.39
  119.5 2.6 copy-start.40
  119.5 2.6 copy-start.41
  130.9 5.8 %copy-start.2 = (f32[40,2048]{1,0:T(8,128)S(1)}, f32[40,2048]{1,0:T(8,128)}, u32[]{:S(2)}) copy-start(f32[40,2048]{1,0:T(8,128)} %get-tuple-element.22) | copy-start | bytes 983044
  138.3 2.8 copy-start.91
  141.0 5.2 %copy-start.97 = (pred[8,128]{1,0:T(8,128)(4,1)S(1)}, pred[8,128]{1,0:T(8,128)(4,1)}, u32[]{:S(2)}) copy-start(pred[8,128]{1,0:T(8,128)(4,1)} %copy-done.96) | copy-start | bytes 3076
  141.0 5.2 %copy-start.99 = (pred[8,128]{1,0:T(8,128)(4,1)S(1)}, pred[8,128]{1,0:T(8,128)(4,1)}, u32[]{:S(2)}) copy-start(pred[8,128]{1,0:T(8,128)(4,1)} %copy-done.98) | copy-start | bytes 3076
  141.0 6.1 %copy-start.105 = (s32[8]{0:T(128)S(1)}, s32[8]{0:T(128)}, u32[]{:S(2)}) copy-start(s32[8]{0:T(128)} %copy-done.104) | copy-start | bytes 100
  149.3 61.1 %all-to-all-start.1 = ((f32[40,32,128]{2,0,1:T(8,128)}), f32[40,32,128]{2,0,1:T(8,128)}, u32[]{:S(2)}, u32[]{:S(2)}) async-start(f32[40,32,128]{2,0,1:T(8,128)} %scatter_fusion.1), calls=%async_computation.1 | async-start | bytes 1310720 | tf_op jit(solution)/shard_map/all_to_all | solution.py:268
  155.3 2.8 %copy-start.78 = (pred[1,16,4,128]{3,1,2,0:T(8,128)(4,1)S(1)}, pred[1,16,4,128]{3,1,2,0:T(8,128)(4,1)}, u32[]{:S(2)}) copy-start(pred[1,16,4,128]{3,1,2,0:T(8,128)(4,1)} %copy.252) | copy-start | bytes 24580
  155.3 2.8 %copy-start.62 = (s32[1,16,4,128]{3,1,2,0:T(8,128)S(1)}, s32[1,16,4,128]{3,1,2,0:T(8,128)}, u32[]{:S(2)}) copy-start(s32[1,16,4,128]{3,1,2,0:T(8,128)} %copy-done.61) | copy-start | bytes 98308
  155.4 44.8 %copy-start.5 = (f32[40,2048]{1,0:T(8,128)S(1)}, f32[40,2048]{1,0:T(8,128)}, u32[]{:S(2)}) copy-start(f32[40,2048]{1,0:T(8,128)} %get-tuple-element.21) | copy-start | bytes 983044
  155.4 45.7 %copy-start.4 = (f32[40,2048]{1,0:T(8,128)S(1)}, f32[40,2048]{1,0:T(8,128)}, u32[]{:S(2)}) copy-start(f32[40,2048]{1,0:T(8,128)} %get-tuple-element.23) | copy-start | bytes 983044
  155.4 46.7 %copy-start.3 = (f32[40,2048]{1,0:T(8,128)S(1)}, f32[40,2048]{1,0:T(8,128)}, u32[]{:S(2)}) copy-start(f32[40,2048]{1,0:T(8,128)} %get-tuple-element.22) | copy-start | bytes 983044
  158.1 44.1 %copy-start.1 = (f32[40,2048]{1,0:T(8,128)S(1)}, f32[40,2048]{1,0:T(8,128)}, u32[]{:S(2)}) copy-start(f32[40,2048]{1,0:T(8,128)} %get-tuple-element.24) | copy-start | bytes 983044
  207.7 4.5 %copy-start.103 = (pred[8]{0:T(512)(128)(4,1)S(1)}, pred[8]{0:T(512)(128)(4,1)}, u32[]{:S(2)}) copy-start(pred[8]{0:T(512)(128)(4,1)} %get-tuple-element.41) | copy-start | bytes 28
  213.6 4.0 %copy-start.53 = (s32[8192]{0:T(1024)S(1)}, s32[8192]{0:T(1024)}, u32[]{:S(2)}) copy-start(s32[8192]{0:T(1024)} %fusion.104) | copy-start | bytes 98308
  217.6 30.2 %copy-start.84 = (pred[8192]{0:T(1024)(128)(4,1)S(1)}, pred[8192]{0:T(1024)(128)(4,1)}, u32[]{:S(2)}) copy-start(pred[8192]{0:T(1024)(128)(4,1)} %compare_and_fusion) | copy-start | bytes 24580
  260.6 6.6 %copy-start.86 = (pred[1,16,4,128]{3,1,2,0:T(8,128)(4,1)S(1)}, pred[1,16,4,128]{3,1,2,0:T(8,128)(4,1)}, u32[]{:S(2)}) copy-start(pred[1,16,4,128]{3,1,2,0:T(8,128)(4,1)} %copy.257) | copy-start | bytes 24580
  260.6 6.6 %copy-start.88 = (pred[1,16,4,128]{3,1,2,0:T(8,128)(4,1)S(1)}, pred[1,16,4,128]{3,1,2,0:T(8,128)(4,1)}, u32[]{:S(2)}) copy-start(pred[1,16,4,128]{3,1,2,0:T(8,128)(4,1)} %copy.259) | copy-start | bytes 24580
  (65 other events, 120.1 us)
where the time goes:
time: 281 us; the launch traced here: 276 us
  local copies, waits for them, and re-layouts  163 us (58%)
  blocking collectives  41.2 us (15%)
  other arithmetic  34.7 us (12%)
  matrix products  20.9 us (7%)
  starting transfers between devices  13.8 us (5%)
    gather x2, local copies, waits for them, and re-layouts, local(): jnp.take(trace_table, gather_index, axis=1).reshape(4, 10, face_count)  60.4 us
    psum x1, blocking collectives, local(): absorbed.append(lax.psum(totals, 'dom') * norm_factor)  41.2 us
    select_n x2, other arithmetic, local(): jnp.take(trace_table, gather_index, axis=1).reshape(4, 10, face_count)  14.9 us
    all_to_all x2, starting transfers between devices, local(): lax.all_to_all(buffer, 'dom', split_axis=1, concat_axis=1, tiled=True)  13.8 us
    dot_general x2, matrix products, orient_values(): jnp.einsum('tnk,fkx->tfnx', rotate_tables, values, precision=lax.Precisio...  12.4 us
    gather x4, local copies, waits for them, and re-layouts, local(): jnp.take(flat_inner, send_index, axis=1)  10.3 us
    slice x2, local copies, waits for them, and re-layouts, physical_derivative(): gradients[field_index, 0]  9.24 us
    slice x2, local copies, waits for them, and re-layouts, face_flux(): inner_trace[1]  8.19 us
  transfers between devices with their start and end apart: 2, of which 0 were waited for; matrix products, arithmetic and copies ran while one was open for 16% of the time, Pallas kernels for 0%

commit v1 on v0

v1 whole, which is shorter than its diff:
```python
import functools
import math

import jax
import jax.numpy as jnp
import numpy as np
from jax import lax
from jax.experimental import pallas as pl
from jax.experimental.pallas import tpu as pltpu
from jax.sharding import PartitionSpec as P

NMAT = 16


section_decay = (-567301805773.0 / 1357537059087.0, -2404267990393.0 / 2016746695238.0)
section_weight = (1720146321549.0 / 2090206949498.0, 3134564353537.0 / 4481467310338.0)
time_step = 0.002


def mat_product(left, right):
    inner = len(right)
    return [
        [sum((left[i][k] * right[k][j] for k in range(inner))) for j in range(len(right[0]))]
        for i in range(len(left))
    ]


def flipped(matrix):
    return [list(row) for row in zip(*matrix)]


def solve_rows(matrix, right):
    size = len(matrix)
    augmented = [list(matrix[i]) + list(right[i]) for i in range(size)]
    for column in range(size):
        pivot = max(range(column, size), key=lambda r: abs(augmented[r][column]))
        augmented[column], augmented[pivot] = (augmented[pivot], augmented[column])
        leader = augmented[column][column]
        augmented[column] = [value / leader for value in augmented[column]]
        for other in range(size):
            if other != column:
                factor = augmented[other][column]
                if factor != 0.0:
                    augmented[other] = [
                        a - factor * b for a, b in zip(augmented[other], augmented[column])
                    ]
    return [row[size:] for row in augmented]


def identity_rows(size):
    return [[1.0 if i == j else 0.0 for j in range(size)] for i in range(size)]


def dg_tables():
    lattice = [(i, j, k) for i in range(4) for j in range(4 - i) for k in range(4 - i - j)]
    coords = [(i / 3.0, j / 3.0, k / 3.0) for i, j, k in lattice]
    vander = [[x**a * y**b * z**c for a, b, c in lattice] for x, y, z in coords]
    inverse = solve_rows(vander, identity_rows(20))
    gradient_rows = []
    for d in range(3):
        derived = []
        for point in coords:
            row = []
            for powers in lattice:
                if powers[d] == 0:
                    row.append(0.0)
                else:
                    lowered = [powers[0], powers[1], powers[2]]
                    lowered[d] = lowered[d] - 1
                    row.append(
                        powers[d]
                        * point[0] ** lowered[0]
                        * point[1] ** lowered[1]
                        * point[2] ** lowered[2]
                    )
            derived.append(row)
        gradient_rows.extend(mat_product(derived, inverse))
    mono_mass = [
        [
            math.factorial(a + p)
            * math.factorial(b + q)
            * math.factorial(c + r)
            / math.factorial(a + b + c + p + q + r + 3)
            for p, q, r in lattice
        ]
        for a, b, c in lattice
    ]
    mass_matrix = mat_product(mat_product(flipped(inverse), mono_mass), inverse)
    plane_points = [(a, b) for a in range(4) for b in range(4 - a)]
    face_coords = [(a / 3.0, b / 3.0) for a, b in plane_points]
    vander_face = [[x**a * y**b for a, b in plane_points] for x, y in face_coords]
    inverse_face = solve_rows(vander_face, identity_rows(10))
    mono_face = [
        [
            math.factorial(a + p) * math.factorial(b + q) / math.factorial(a + b + p + q + 2)
            for p, q in plane_points
        ]
        for a, b in plane_points
    ]
    face_mass = mat_product(mat_product(flipped(inverse_face), mono_face), inverse_face)
    position = {point: n for n, point in enumerate(lattice)}
    builders = [
        lambda a, b: (a, b, 0),
        lambda a, b: (a, 0, b),
        lambda a, b: (0, a, b),
        lambda a, b: (a, b, 3 - a - b),
    ]
    face_nodes = [[position[builder(a, b)] for a, b in plane_points] for builder in builders]
    surface = [[0.0] * 40 for n in range(20)]
    for f in range(4):
        for n in range(10):
            for m in range(10):
                surface[face_nodes[f][n]][f * 10 + m] = face_mass[n][m]
    lift_matrix = solve_rows(mass_matrix, surface)
    rotations = []
    for t in range(3):
        mapping = []
        for a, b in plane_points:
            triple = (b, a, 3 - a - b)
            for s in range(t):
                triple = (triple[1], triple[2], triple[0])
            mapping.append(plane_points.index((triple[0], triple[1])))
        rotations.append(mapping)
    return (gradient_rows, lift_matrix, face_nodes, rotations)


def peer_offsets(half_span):
    return [j - half_span if j < half_span else j - half_span + 1 for j in range(2 * half_span)]


LANES = 128
SUB = 8
PAD = 24
SLOT = 16
CHUNK = 256
MESH = pl.DeviceIdType.MESH


def operator_tables():
    grad_rows, lift_rows, face_nodes, rotations = dg_tables()
    grads = np.array(grad_rows, dtype=np.float64).reshape(3, 20, 20)
    volume = np.zeros((4 * PAD, 4 * PAD))
    for a in range(3):
        volume[0:20, a * PAD : a * PAD + 20] = -grads[a]
        volume[(a + 1) * PAD : (a + 1) * PAD + 20, 3 * PAD : 3 * PAD + 20] = grads[a]
    lift_node_major = np.array(
        [[row[f * 10 + m] for m in range(10) for f in range(4)] for row in lift_rows]
    )
    lift = np.zeros((4 * PAD, 160))
    for field in range(4):
        lift[field * PAD : field * PAD + 20, field * 40 : field * 40 + 40] = lift_node_major
    return (volume, lift, face_nodes, rotations)


def split_table(table):
    single = jnp.asarray(table, dtype=jnp.float32)
    high = single.astype(jnp.bfloat16)
    low = (single - high.astype(jnp.float32)).astype(jnp.bfloat16)
    return (high, low)


def split_dot(high, low, values):
    value_high = values.astype(jnp.bfloat16)
    value_low = (values - value_high.astype(jnp.float32)).astype(jnp.bfloat16)
    dot = functools.partial(jnp.dot, preferred_element_type=jnp.float32)
    return dot(high, value_high) + (dot(high, value_low) + dot(low, value_high))


def lane_pick(row, lanes):
    spread = jnp.broadcast_to(row, lanes.shape)
    return jnp.take_along_axis(spread, lanes, axis=1, mode="promise_in_bounds")


def step_kernel(
    devices,
    face_nodes,
    rotations,
    sol,
    reg,
    geo,
    nrm,
    fsc,
    imp,
    nbr,
    ori,
    mat,
    snd,
    vol_high,
    vol_low,
    lift_high,
    lift_low,
    sol_out,
    reg_out,
    tot_out,
    xd,
    tab,
    hd,
    acc,
    nd,
    n2,
    code_d,
    orient_d,
    mat_d,
    half_scale,
    reflect_d,
    loss_d,
    yv,
    vol,
    fl,
    send_buf,
    recv_buf,
    send_sem,
    recv_sem,
):
    elems = sol.shape[2]
    eb_count = elems // LANES
    rows = 4 * eb_count
    groups = rows // SUB
    blocks = snd.shape[0]
    materials = imp.shape[0]
    offsets = peer_offsets(blocks // 2)
    me = lax.axis_index("dom")
    peers = [me + o for o in offsets]
    valid = [(p >= 0) & (p < devices) for p in peers]

    recv_buf[...] = jnp.zeros_like(recv_buf)
    barrier = pltpu.get_barrier_semaphore()
    for j in range(blocks):

        @pl.when(valid[j])
        def _():
            pl.semaphore_signal(barrier, inc=1, device_id=(peers[j],), device_id_type=MESH)

    for i in range(3):
        n2[i, 0:4, :] = nrm[i]
        n2[i, 4:8, :] = nrm[i]
    for eb in range(eb_count):
        lanes = slice(eb * LANES, (eb + 1) * LANES)
        spread = pl.ds(eb, 4, stride=eb_count)
        for i in range(3):
            nd[pl.ds(i * rows + eb, 4, stride=eb_count), :] = nrm[i, :, lanes]
        half_scale[spread, :] = 0.5 * fsc[:, lanes]
        code_d[spread, :] = nbr[:, lanes]
        orient_d[spread, :] = ori[:, lanes]
        mat_d[spread, :] = mat[:, lanes]

    def reflect_rows(g, carry):
        at = pl.ds(pl.multiple_of(g * SUB, SUB), SUB)
        kind = mat_d[at, :]
        picked = jnp.zeros((SUB, LANES), jnp.float32)
        for m in range(materials):
            picked = jnp.where(kind == m, imp[m], picked)
        reflect = (picked - 1.0) / (picked + 1.0)
        reflect_d[at, :] = reflect
        loss = 0.5 * half_scale[at, :] * (1.0 - reflect * reflect)
        loss_d[at, :] = jnp.where(code_d[at, :] < 0, loss, 0.0)
        return carry

    lax.fori_loop(0, groups, reflect_rows, 0)
    for block in range(4):
        yv[block * PAD + SLOT : (block + 1) * PAD, :] = jnp.zeros((PAD - SLOT, elems), jnp.float32)

    def copy_out(section, j):
        return pltpu.make_async_remote_copy(
            src_ref=send_buf.at[pl.ds((section * blocks + j) * SLOT, SLOT), :],
            dst_ref=recv_buf.at[pl.ds((section * blocks + blocks - 1 - j) * SLOT, SLOT), :],
            send_sem=send_sem.at[section, j],
            recv_sem=recv_sem.at[section, blocks - 1 - j],
            device_id=(peers[j],),
            device_id_type=MESH,
        )

    def copy_in(section, j):
        return pltpu.make_async_remote_copy(
            src_ref=send_buf.at[pl.ds((section * blocks + j) * SLOT, SLOT), :],
            dst_ref=recv_buf.at[pl.ds((section * blocks + j) * SLOT, SLOT), :],
            send_sem=send_sem.at[section, j],
            recv_sem=recv_sem.at[section, j],
            device_id=(peers[j],),
            device_id_type=MESH,
        )

    def gather_local(codes):
        high = [code >> 7 for code in codes]
        low = [code & (LANES - 1) for code in codes]
        zero = jnp.zeros((SUB, LANES), jnp.float32)

        def one_row(k, values):
            values = [list(v) for v in values]
            hit = [h == k for h in high]
            for n in range(10):
                row = tab[pl.ds(n * rows + k, 1), :]
                for g in range(len(codes)):
                    values[g][n] = jnp.where(hit[g], lane_pick(row, low[g]), values[g][n])
            return tuple(tuple(v) for v in values)

        def some_rows(q, values):
            for r in range(4):
                values = one_row(q * 4 + r, values)
            return values

        start = tuple(tuple(zero for _ in range(10)) for _ in codes)
        return lax.fori_loop(0, rows // 4, some_rows, start)

    for section in range(2):
        sol_in = sol if section == 0 else sol_out
        reg_in = reg if section == 0 else reg_out

        for field in range(4):
            for first in range(0, 20, SUB):
                count = min(SUB, 20 - first)
                for eb in range(eb_count):
                    place = pl.ds((field * 20 + first) * eb_count + eb, count, stride=eb_count)
                    xd[place, :] = sol_in[
                        field, first : first + count, eb * LANES : (eb + 1) * LANES
                    ]

        for f in range(4):
            normal = [nd[i * rows + f * eb_count : i * rows + (f + 1) * eb_count, :] for i in range(3)]
            for n in range(10):
                node = face_nodes[f][n]
                press, u, v, w = [
                    xd[(field * 20 + node) * eb_count : (field * 20 + node + 1) * eb_count, :]
                    for field in range(4)
                ]
                un = normal[0] * u + normal[1] * v + normal[2] * w
                spot = slice(n * rows + f * eb_count, n * rows + (f + 1) * eb_count)
                tab[spot, :] = press + un
                hd[spot, :] = un - press

        outgoing = gather_local([snd[...]])[0]
        for n in range(10):
            place = pl.ds(section * blocks * SLOT + n, blocks, stride=SLOT)
            send_buf[place, :] = outgoing[n]
        for n in range(10, SLOT):
            place = pl.ds(section * blocks * SLOT + n, blocks, stride=SLOT)
            send_buf[place, :] = jnp.zeros((blocks, LANES), jnp.float32)

        if section == 0:
            expected = sum(v.astype(jnp.int32) for v in valid)
            pl.semaphore_wait(barrier, expected)
        for j in range(blocks):

            @pl.when(valid[j])
            def _():
                copy_out(section, j).start()

        def loss_rows(g, sums):
            at = pl.multiple_of(g * SUB, SUB)
            total = jnp.zeros((SUB, LANES), jnp.float32)
            for n in range(10):
                value = tab[pl.ds(pl.multiple_of(n * rows + at, SUB), SUB), :]
                total = total + value * value
            total = total * loss_d[pl.ds(at, SUB), :]
            kind = mat_d[pl.ds(at, SUB), :]
            return tuple(s + jnp.where(kind == m, total, 0.0) for m, s in enumerate(sums))

        sums = lax.fori_loop(
            0,
            groups,
            loss_rows,
            tuple(jnp.zeros((SUB, LANES), jnp.float32) for _ in range(materials)),
        )
        for m in range(materials):
            tot_out[section * materials + m : section * materials + m + 1, :] = jnp.sum(
                sums[m], axis=0, keepdims=True
            )

        def volume_chunk(c, carry):
            at = pl.ds(pl.multiple_of(c * CHUNK, CHUNK), CHUNK)
            velocity = [sol_in[i + 1, :, at] for i in range(3)]
            metric = geo[:, at]
            for a in range(3):
                yv[a * PAD : a * PAD + 20, at] = (
                    metric[a : a + 1] * velocity[0]
                    + metric[3 + a : 4 + a] * velocity[1]
                    + metric[6 + a : 7 + a] * velocity[2]
                )
            yv[3 * PAD : 3 * PAD + 20, at] = sol_in[0, :, at]
            out = split_dot(vol_high[...], vol_low[...], yv[:, at])
            vol[0:PAD, at] = out[0:PAD]
            grads = [out[(a + 1) * PAD : (a + 2) * PAD] for a in range(3)]
            for i in range(3):
                vol[(i + 1) * PAD : (i + 2) * PAD, at] = -(
                    metric[3 * i : 3 * i + 1] * grads[0]
                    + metric[3 * i + 1 : 3 * i + 2] * grads[1]
                    + metric[3 * i + 2 : 3 * i + 3] * grads[2]
                )
            return carry

        lax.fori_loop(0, elems // CHUNK, volume_chunk, 0)

        def local_pair(q, carry):
            starts = [pl.multiple_of(q * 2 * SUB + g * SUB, SUB) for g in range(2)]
            found = gather_local([code_d[pl.ds(at, SUB), :] for at in starts])
            for at, values in zip(starts, found):
                for n in range(10):
                    acc[pl.ds(pl.multiple_of(n * rows + at, SUB), SUB), :] = values[n]
            return carry

        lax.fori_loop(0, groups // 2, local_pair, 0)

        for j in range(blocks):

            @pl.when(valid[j])
            def _():
                copy_in(section, j).wait_recv()

        def finish_rows(g, carry):
            at = pl.multiple_of(g * SUB, SUB)
            here = pl.ds(at, SUB)
            code = code_d[here, :]
            high = code >> 7
            low = code & (LANES - 1)
            planes = [pl.ds(pl.multiple_of(n * rows + at, SUB), SUB) for n in range(10)]
            values = [acc[planes[n], :] for n in range(10)]
            for j in range(blocks):
                hit = high == rows + j
                for n in range(10):
                    spot = (section * blocks + j) * SLOT + n
                    row = recv_buf[spot : spot + 1, :]
                    values[n] = jnp.where(hit, lane_pick(row, low), values[n])
            turn = orient_d[here, :]
            wall = code < 0
            reflect = reflect_d[here, :]
            scale = half_scale[here, :]
            for n in range(10):
                seen = jnp.where(
                    turn == 0,
                    values[rotations[0][n]],
                    jnp.where(turn == 1, values[rotations[1][n]], values[rotations[2][n]]),
                )
                seen = jnp.where(wall, reflect * tab[planes[n], :], seen)
                hd[planes[n], :] = scale * (hd[planes[n], :] + seen)
            return carry

        lax.fori_loop(0, groups, finish_rows, 0)

        for eb in range(eb_count):
            lanes = slice(eb * LANES, (eb + 1) * LANES)
            normal = [n2[i, :, lanes] for i in range(3)]
            for kb in range(5):
                flux = hd[pl.ds(kb * SUB * eb_count + eb, SUB, stride=eb_count), :]
                fl[kb * SUB : (kb + 1) * SUB, lanes] = flux
                for i in range(3):
                    first = 40 * (i + 1) + kb * SUB
                    fl[first : first + SUB, lanes] = -normal[i] * flux

        def update_chunk(c, carry):
            at = pl.ds(pl.multiple_of(c * CHUNK, CHUNK), CHUNK)
            lifted = split_dot(lift_high[...], lift_low[...], fl[:, at])
            for field in range(4):
                rhs = lifted[field * PAD : field * PAD + 20] + vol[field * PAD : field * PAD + 20, at]
                new = section_decay[section] * reg_in[field, :, at] + time_step * rhs
                sol_out[field, :, at] = sol_in[field, :, at] + section_weight[section] * new
                reg_out[field, :, at] = new
            return carry

        lax.fori_loop(0, elems // CHUNK, update_chunk, 0)

    for section in range(2):
        for j in range(blocks):

            @pl.when(valid[j])
            def _():
                copy_out(section, j).wait_send()


def local(
    solution,
    register,
    geometry,
    normals,
    face_scale,
    impedance,
    neighbour,
    orientation,
    wall_material,
    send_faces,
):
    volume, lift, face_nodes, rotations = operator_tables()
    tables = split_table(volume) + split_table(lift)
    elems = solution.shape[2]
    rows = 4 * elems // LANES
    blocks = send_faces.shape[0]
    materials = impedance.shape[0]
    devices = lax.axis_size("dom")
    f32, i32 = (jnp.float32, jnp.int32)
    vmem = pl.BlockSpec(memory_space=pltpu.VMEM)
    smem = pl.BlockSpec(memory_space=pltpu.SMEM)
    out, register_out, totals = pl.pallas_call(
        functools.partial(step_kernel, devices, face_nodes, rotations),
        out_shape=(
            jax.ShapeDtypeStruct(solution.shape, f32),
            jax.ShapeDtypeStruct(register.shape, f32),
            jax.ShapeDtypeStruct((2 * materials, LANES), f32),
        ),
        in_specs=[vmem] * 5 + [smem] + [vmem] * 8,
        out_specs=(vmem, vmem, vmem),
        scratch_shapes=[
            pltpu.VMEM((20 * rows, LANES), f32),
            pltpu.VMEM((10 * rows, LANES), f32),
            pltpu.VMEM((10 * rows, LANES), f32),
            pltpu.VMEM((10 * rows, LANES), f32),
            pltpu.VMEM((3 * rows, LANES), f32),
            pltpu.VMEM((3, SUB, elems), f32),
            pltpu.VMEM((rows, LANES), i32),
            pltpu.VMEM((rows, LANES), i32),
            pltpu.VMEM((rows, LANES), i32),
            pltpu.VMEM((rows, LANES), f32),
            pltpu.VMEM((rows, LANES), f32),
            pltpu.VMEM((rows, LANES), f32),
            pltpu.VMEM((4 * PAD, elems), f32),
            pltpu.VMEM((4 * PAD, elems), f32),
            pltpu.VMEM((160, elems), f32),
            pltpu.VMEM((2 * blocks * SLOT, LANES), f32),
            pltpu.VMEM((2 * blocks * SLOT, LANES), f32),
            pltpu.SemaphoreType.DMA((2, blocks)),
            pltpu.SemaphoreType.DMA((2, blocks)),
        ],
        compiler_params=pltpu.CompilerParams(
            collective_id=0, has_side_effects=True, vmem_limit_bytes=40 * 1024 * 1024
        ),
    )(
        solution,
        register,
        geometry,
        normals,
        face_scale,
        impedance,
        neighbour,
        orientation,
        wall_material,
        send_faces,
        *tables,
    )
    per_section = jnp.sum(totals, axis=1).reshape(2, materials)
    absorbed = lax.psum(per_section, "dom") * (NMAT / (devices * elems))
    return (out, register_out, absorbed)


def solution(mesh):
    in_specs = (
        P(None, None, "dom"),
        P(None, None, "dom"),
        P(None, "dom"),
        P(None, None, "dom"),
        P(None, "dom"),
        P(),
        P(None, "dom"),
        P(None, "dom"),
        P(None, "dom"),
        P("dom", None),
    )
    out_specs = (P(None, None, "dom"), P(None, None, "dom"), P())
    return jax.shard_map(local, mesh=mesh, in_specs=in_specs, out_specs=out_specs, check_vma=False)
```

time: 281 us -> 84.4 us (0.30); the launches traced: 276 us -> 84.2 us
  local copies, waits for them, and re-layouts: 163 us -> 5.02 us
  Pallas kernels: 0 us -> 36.3 us
  other arithmetic: 34.7 us -> 0.67 us
  matrix products: 20.9 us -> 0 us
  starting transfers between devices: 13.8 us -> 0 us
    gather x12 -> x0, local copies, waits for them, and re-layouts: 80.7 us -> none  [the longest x2 60.4 us: local(): jnp.take(trace_table, gather_index, axis=1).reshape(4, 10, face_count)]
    pallas_call x0 -> x1, Pallas kernels: none -> 36.3 us  [local(): pl.pallas_call(functools.partial(step_kernel, devices, face_nodes, rotati...]
    dot_general x6 -> x0, matrix products: 20.9 us -> none  [the longest x2 12.4 us: orient_values(): jnp.einsum('tnk,fkx->tfnx', rotate_tables, values, precision=lax.Precisio...]
    slice x5 -> x0, local copies, waits for them, and re-layouts: 18.1 us -> none  [the longest x2 9.24 us: physical_derivative(): gradients[field_index, 0]]
    squeeze x16 -> x0, local copies, waits for them, and re-layouts: 17.5 us -> none  [the longest x4 4.83 us: face_flux(): inner_trace[2]]
    select_n x8 -> x0, other arithmetic: 15.6 us -> none  [the longest x2 14.9 us: local(): jnp.take(trace_table, gather_index, axis=1).reshape(4, 10, face_count)]
    all_to_all x2 -> x0, starting transfers between devices: 13.8 us -> none  [local(): lax.all_to_all(buffer, 'dom', split_axis=1, concat_axis=1, tiled=True)]
    another operation x14 -> x0, local copies, waits for them, and re-layouts: 12 us -> none  [the longest x4 7.94 us: local(): flat_inner = inner_trace.reshape(40, face_count)]
  transfers between devices with their start and end apart: 2 -> 0, of which waited for: 0 -> 0; matrix products, arithmetic and copies ran while one was open for 16% -> 0% of each run, Pallas kernels for 0% -> 0%
where the time goes in v1:
time: 84.4 us; the launch traced here: 84.2 us
  blocking collectives  41.3 us (49%)
  Pallas kernels  36.3 us (43%)
  local copies, waits for them, and re-layouts  5.02 us (6%)
    psum x1, blocking collectives, local(): absorbed = lax.psum(per_section, 'dom') * (NMAT / (devices * elems))  41.3 us
    pallas_call x1, Pallas kernels, local(): pl.pallas_call(functools.partial(step_kernel, devices, face_nodes, rotati...  36.3 us
    unnamed x30, local copies, waits for them, and re-layouts  4.94 us

profile of v1, /device:TPU:0, one launch (start us, length us, event | category | flops | bytes accessed | tf_op | source)
XLA Modules:
  0.0 84.2 jit_solution(4474734177947318309)
XLA Ops:
  0.6 0.0 copy-start.12
  0.6 1.5 %copy.15.sol = f32[4,20,2048]{2,1,0:T(8,128)S(1)} copy(f32[4,20,2048]{2,0,1:T(4,128)} %param.12) | data formatting | bytes 1310720 | tf_op args[0]
  2.2 0.0 copy-done.12
  2.2 0.0 copy-start
  2.2 0.0 copy-start.1
  2.2 0.0 copy-start.2
  2.2 0.0 copy-start.3
  2.2 0.0 copy-start.4
  2.2 0.0 copy-start.5
  2.3 0.0 copy-start.6
  2.3 0.0 copy-start.7
  2.3 0.0 copy-start.8
  2.3 0.0 copy-start.9
  2.3 0.0 copy-start.10
  2.3 0.0 copy-start.11
  2.3 0.4 copy.16.reg
  2.7 0.4 copy-done
  3.1 0.1 copy-done.1
  3.1 0.0 copy-done.2
  3.2 0.0 copy-done.3
  3.2 0.0 copy-done.4
  3.2 0.0 copy-done.5
  3.2 0.0 copy-done.6
  3.2 0.0 copy-done.7
  3.2 0.0 copy-done.8
  3.2 0.0 copy-done.9
  3.2 0.0 copy-done.10
  3.2 0.0 copy-done.11
  3.2 36.3 %shard_map.139 = (f32[4,20,2048]{2,1,0:T(8,128)S(1)}, f32[4,20,2048]{2,1,0:T(8,128)S(1)}, f32[32,128]{1,0:T(8,128)S(1)}) custom-call(f32[4,20,2048]{2,1,0:T(8,128)S(1)} %copy.15.sol, f32[4,20,2048]{2,1,0:T(8,128)S(1)} %copy.16.reg, f32[9,2048]{1,0:T(8,128)S(1)} %copy-done, f32[3,4,2048]{2,1,0:T(4,128)S(1)} %copy-done.1, f32[4,2048]{1,0:T(4,128)S(1)} %copy-done.4, ...), custom_call_target="tpu_custom_call" | custom-call | tf_op jit(solution)/shard_map/pallas_call | solution.py:491
  39.5 1.3 %copy.17 = f32[4,20,2048]{2,0,1:T(4,128)} copy(f32[4,20,2048]{2,1,0:T(8,128)S(1)} %get-tuple-element.9) | data formatting | bytes 1310720
  40.8 0.1 reduce_sum.9
  40.9 0.1 reshape.9
  41.0 41.3 %psum.7 = f32[2,16]{1,0:T(2,128)S(1)} all-reduce(f32[2,16]{1,0:T(2,128)S(1)} %reshape.9), channel_id=1, replica_groups=mesh['dom'=32] {'dom'}, use_global_device_ids=true, to_apply=%region_1.0 | all-reduce | flops 32 | bytes 256 | tf_op jit(solution)/shard_map/psum | solution.py:538
  82.3 0.6 broadcast_multiply_fusion
  82.9 1.3 %copy.18 = f32[4,20,2048]{2,0,1:T(4,128)} copy(f32[4,20,2048]{2,1,0:T(8,128)S(1)} %get-tuple-element.10) | data formatting | bytes 1310720
Async XLA Ops:
  0.6 1.5 %copy-start.12 = (f32[4,20,2048]{2,0,1:T(4,128)S(1)}, f32[4,20,2048]{2,0,1:T(4,128)}, u32[]{:S(2)}) copy-start(f32[4,20,2048]{2,0,1:T(4,128)} %param.13) | copy-start | bytes 1966084
  2.2 0.9 %copy-start = (f32[9,2048]{1,0:T(8,128)S(1)}, f32[9,2048]{1,0:T(8,128)}, u32[]{:S(2)}) copy-start(f32[9,2048]{1,0:T(8,128)} %geo.1) | copy-start | bytes 221188
  2.2 0.9 %copy-start.1 = (f32[3,4,2048]{2,1,0:T(4,128)S(1)}, f32[3,4,2048]{2,1,0:T(4,128)}, u32[]{:S(2)}) copy-start(f32[3,4,2048]{2,1,0:T(4,128)} %nrm.1) | copy-start | bytes 294916
  2.2 0.9 %copy-start.2 = (bf16[96,160]{1,0:T(8,128)(2,1)S(1)}, bf16[96,160]{1,0:T(8,128)(2,1)}, u32[]{:S(2)}) copy-start(bf16[96,160]{1,0:T(8,128)(2,1)} %constant.18.lift_low) | copy-start | bytes 92164
  2.2 0.9 %copy-start.3 = (bf16[96,160]{1,0:T(8,128)(2,1)S(1)}, bf16[96,160]{1,0:T(8,128)(2,1)}, u32[]{:S(2)}) copy-start(bf16[96,160]{1,0:T(8,128)(2,1)} %constant.15.lift_high) | copy-start | bytes 92164
  2.2 0.9 %copy-start.4 = (f32[4,2048]{1,0:T(4,128)S(1)}, f32[4,2048]{1,0:T(4,128)}, u32[]{:S(2)}) copy-start(f32[4,2048]{1,0:T(4,128)} %fsc.1) | copy-start | bytes 98308
  2.2 0.9 %copy-start.5 = (s32[4,2048]{1,0:T(4,128)S(1)}, s32[4,2048]{1,0:T(4,128)}, u32[]{:S(2)}) copy-start(s32[4,2048]{1,0:T(4,128)} %nbr.1) | copy-start | bytes 98308
  2.3 0.9 %copy-start.6 = (s32[4,2048]{1,0:T(4,128)S(1)}, s32[4,2048]{1,0:T(4,128)}, u32[]{:S(2)}) copy-start(s32[4,2048]{1,0:T(4,128)} %ori.1) | copy-start | bytes 98308
  2.3 0.9 %copy-start.7 = (s32[4,2048]{1,0:T(4,128)S(1)}, s32[4,2048]{1,0:T(4,128)}, u32[]{:S(2)}) copy-start(s32[4,2048]{1,0:T(4,128)} %mat.1) | copy-start | bytes 98308
  2.3 0.9 %copy-start.8 = (bf16[96,96]{1,0:T(8,128)(2,1)S(1)}, bf16[96,96]{1,0:T(8,128)(2,1)}, u32[]{:S(2)}) copy-start(bf16[96,96]{1,0:T(8,128)(2,1)} %constant.14.vol_low) | copy-start | bytes 55300
  2.3 0.9 %copy-start.9 = (bf16[96,96]{1,0:T(8,128)(2,1)S(1)}, bf16[96,96]{1,0:T(8,128)(2,1)}, u32[]{:S(2)}) copy-start(bf16[96,96]{1,0:T(8,128)(2,1)} %constant.11.vol_high) | copy-start | bytes 55300
  2.3 0.9 %copy-start.10 = (s32[8,128]{1,0:T(8,128)S(1)}, s32[8,128]{1,0:T(8,128)}, u32[]{:S(2)}) copy-start(s32[8,128]{1,0:T(8,128)} %snd.1) | copy-start | bytes 12292
  2.3 0.9 %copy-start.11 = (f32[16]{0:T(128)S(1)}, f32[16]{0:T(128)}, u32[]{:S(2)}) copy-start(f32[16]{0:T(128)} %imp.1) | copy-start | bytes 196

commit v2 on v1

--- a/solution.py
+++ b/solution.py
@@ -209,8 +209,14 @@
     fl,
     send_buf,
     recv_buf,
+    hot,
+    table,
+    part_sent,
+    part_got,
     send_sem,
     recv_sem,
+    part_send_sem,
+    part_recv_sem,
 ):
     elems = sol.shape[2]
     eb_count = elems // LANES
@@ -222,14 +228,22 @@
     me = lax.axis_index("dom")
     peers = [me + o for o in offsets]
     valid = [(p >= 0) & (p < devices) for p in peers]
+    stages = devices.bit_length() - 1
+    assert devices == 1 << stages
+    partners = [me + (1 << s) - (2 << s) * ((me // (1 << s)) % 2) for s in range(stages)]
+    far = [s for s in range(stages) if 1 << s > blocks // 2]
 
     recv_buf[...] = jnp.zeros_like(recv_buf)
+    send_buf[...] = jnp.zeros_like(send_buf)
     barrier = pltpu.get_barrier_semaphore()
     for j in range(blocks):
 
         @pl.when(valid[j])
         def _():
             pl.semaphore_signal(barrier, inc=1, device_id=(peers[j],), device_id_type=MESH)
+
+    for s in far:
+        pl.semaphore_signal(barrier, inc=1, device_id=(partners[s],), device_id_type=MESH)
 
     for i in range(3):
         n2[i, 0:4, :] = nrm[i]
@@ -280,27 +294,90 @@
             device_id_type=MESH,
         )
 
-    def gather_local(codes):
-        high = [code >> 7 for code in codes]
-        low = [code & (LANES - 1) for code in codes]
-        zero = jnp.zeros((SUB, LANES), jnp.float32)
-
-        def one_row(k, values):
-            values = [list(v) for v in values]
-            hit = [h == k for h in high]
-            for n in range(10):
-                row = tab[pl.ds(n * rows + k, 1), :]
-                for g in range(len(codes)):
-                    values[g][n] = jnp.where(hit[g], lane_pick(row, low[g]), values[g][n])
-            return tuple(tuple(v) for v in values)
-
-        def some_rows(q, values):
-            for r in range(4):
-                values = one_row(q * 4 + r, values)
-            return values
-
-        start = tuple(tuple(zero for _ in range(10)) for _ in codes)
-        return lax.fori_loop(0, rows // 4, some_rows, start)
+    def hot_rows(codes, column):
+        low = jnp.broadcast_to(codes & (LANES - 1), (LANES, LANES))
+        one = jnp.where(lax.broadcasted_iota(jnp.int32, (LANES, LANES), 0) == low, 1.0, 0.0)
+        one = one.astype(jnp.bfloat16)
+        hot[0:LANES, pl.ds(column, LANES)] = one
+        hot[LANES : 2 * LANES, pl.ds(column, LANES)] = one
+
+    def hot_face_row(r, carry):
+        hot_rows(code_d[pl.ds(r, 1), :], pl.multiple_of(r * LANES, LANES))
+        return carry
+
+    lax.fori_loop(0, rows, hot_face_row, 0)
+    for j in range(blocks):
+        hot_rows(snd[j : j + 1, :], (rows + j) * LANES)
+
+    def fill_table():
+        for pair in range(rows // 2):
+            value = jnp.concatenate(
+                [tab[pl.ds(pair * 2 + h, SUB, stride=rows), :] for h in range(2)], axis=0
+            )
+            put_split(pair * SLOT, value)
+        for q in range(groups):
+            value = jnp.concatenate(
+                [tab[n * rows + q * SUB : n * rows + (q + 1) * SUB, :] for n in (8, 9)], axis=0
+            )
+            put_split(rows * SUB + q * SLOT, value)
+
+    def put_split(first, value):
+        high = value.astype(jnp.bfloat16)
+        table[first : first + SLOT, 0:LANES] = high
+        table[first : first + SLOT, LANES : 2 * LANES] = (
+            value - high.astype(jnp.float32)
+        ).astype(jnp.bfloat16)
+
+    def pick_tile(column, codes):
+        product = jnp.dot(
+            table[...], hot[:, pl.ds(column, 2 * LANES)], preferred_element_type=jnp.float32
+        )
+        found = []
+        for h in range(2):
+            lanes = slice(h * LANES, (h + 1) * LANES)
+            high = jnp.broadcast_to(codes[h] >> 7, (SUB, LANES))
+            main = jnp.zeros((SUB, LANES), jnp.float32)
+            for k in range(rows):
+                main = jnp.where(high == k, product[k * SUB : (k + 1) * SUB, lanes], main)
+            within = high - lax.broadcasted_iota(jnp.int32, (SUB, LANES), 0)
+            rest = [jnp.zeros((SUB, LANES), jnp.float32) for _ in range(2)]
+            for q in range(groups):
+                hit = within == q * SUB
+                for r in range(2):
+                    first = rows * SUB + q * SLOT + r * SUB
+                    rest[r] = jnp.where(hit, product[first : first + SUB, lanes], rest[r])
+            found.append((main, [jnp.sum(r, axis=0, keepdims=True) for r in rest]))
+        return found
+
+    def part_copy(s):
+        return pltpu.make_async_remote_copy(
+            src_ref=part_sent.at[s],
+            dst_ref=part_got.at[s],
+            send_sem=part_send_sem.at[s],
+            recv_sem=part_recv_sem.at[s],
+            device_id=(partners[s],),
+            device_id_type=MESH,
+        )
+
+    def advance(s):
+        if s >= stages:
+            return
+        part_copy(s).wait_recv()
+        total = part_sent[s] + part_got[s]
+        if s + 1 < stages:
+            part_sent[s + 1] = total
+            part_copy(s + 1).start()
+            return
+        ones = jnp.ones((SUB, LANES), jnp.float32)
+        for section in range(2):
+            sums = lax.dot_general(
+                ones,
+                total[section * materials : (section + 1) * materials],
+                (((1,), (1,)), ((), ())),
+                precision=lax.Precision.HIGHEST,
+                preferred_element_type=jnp.float32,
+            )
+            tot_out[section : section + 1, :] = sums[0:1] * (NMAT / (devices * elems))
 
     for section in range(2):
         sol_in = sol if section == 0 else sol_out
@@ -328,16 +405,24 @@
                 tab[spot, :] = press + un
                 hd[spot, :] = un - press
 
-        outgoing = gather_local([snd[...]])[0]
-        for n in range(10):
-            place = pl.ds(section * blocks * SLOT + n, blocks, stride=SLOT)
-            send_buf[place, :] = outgoing[n]
-        for n in range(10, SLOT):
-            place = pl.ds(section * blocks * SLOT + n, blocks, stride=SLOT)
-            send_buf[place, :] = jnp.zeros((blocks, LANES), jnp.float32)
+        fill_table()
+
+        def send_pair(q, carry):
+            first = q * 2
+            column = pl.multiple_of((rows + first) * LANES, 2 * LANES)
+            found = pick_tile(column, [snd[pl.ds(first + h, 1), :] for h in range(2)])
+            for h in range(2):
+                at = pl.multiple_of((section * blocks + first + h) * SLOT, SLOT)
+                main, rest = found[h]
+                send_buf[pl.ds(at, SUB), :] = main
+                for r in range(2):
+                    send_buf[pl.ds(at + SUB + r, 1), :] = rest[r]
+            return carry
+
+        lax.fori_loop(0, blocks // 2, send_pair, 0)
 
         if section == 0:
-            expected = sum(v.astype(jnp.int32) for v in valid)
+            expected = len(far) + sum(v.astype(jnp.int32) for v in valid)
             pl.semaphore_wait(barrier, expected)
         for j in range(blocks):
 
@@ -362,9 +447,10 @@
             tuple(jnp.zeros((SUB, LANES), jnp.float32) for _ in range(materials)),
         )
         for m in range(materials):
-            tot_out[section * materials + m : section * materials + m + 1, :] = jnp.sum(
-                sums[m], axis=0, keepdims=True
-            )
+            spot = section * materials + m
+            part_sent[0, spot : spot + 1, :] = jnp.sum(sums[m], axis=0, keepdims=True)
+        if section == 1:
+            part_copy(0).start()
 
         def volume_chunk(c, carry):
             at = pl.ds(pl.multiple_of(c * CHUNK, CHUNK), CHUNK)
@@ -391,14 +477,24 @@
         lax.fori_loop(0, elems // CHUNK, volume_chunk, 0)
 
         def local_pair(q, carry):
-            starts = [pl.multiple_of(q * 2 * SUB + g * SUB, SUB) for g in range(2)]
-            found = gather_local([code_d[pl.ds(at, SUB), :] for at in starts])
-            for at, values in zip(starts, found):
-                for n in range(10):
-                    acc[pl.ds(pl.multiple_of(n * rows + at, SUB), SUB), :] = values[n]
+            first = q * 2
+            column = pl.multiple_of(first * LANES, 2 * LANES)
+            found = pick_tile(column, [code_d[pl.ds(first + h, 1), :] for h in range(2)])
+            for h in range(2):
+                main, rest = found[h]
+                acc[pl.ds(first + h, SUB, stride=rows), :] = main
+                for r in range(2):
+                    acc[pl.ds((SUB + r) * rows + first + h, 1), :] = rest[r]
             return carry
 
-        lax.fori_loop(0, groups // 2, local_pair, 0)
+        if section == 0:
+            lax.fori_loop(0, rows // 2, local_pair, 0)
+        else:
+            advance(0)
+            lax.fori_loop(0, rows // 4, local_pair, 0)
+            advance(1)
+            lax.fori_loop(rows // 4, rows // 2, local_pair, 0)
+            advance(2)
 
         for j in range(blocks):
 
@@ -435,6 +531,8 @@
             return carry
 
         lax.fori_loop(0, groups, finish_rows, 0)
+        if section == 1:
+            advance(3)
 
         for eb in range(eb_count):
             lanes = slice(eb * LANES, (eb + 1) * LANES)
@@ -446,6 +544,9 @@
                     first = 40 * (i + 1) + kb * SUB
                     fl[first : first + SUB, lanes] = -normal[i] * flux
 
+        if section == 1:
+            advance(4)
+
         def update_chunk(c, carry):
             at = pl.ds(pl.multiple_of(c * CHUNK, CHUNK), CHUNK)
             lifted = split_dot(lift_high[...], lift_low[...], fl[:, at])
@@ -457,6 +558,11 @@
             return carry
 
         lax.fori_loop(0, elems // CHUNK, update_chunk, 0)
+
+    for s in range(5, stages):
+        advance(s)
+    for s in range(stages):
+        part_copy(s).wait_send()
 
     for section in range(2):
         for j in range(blocks):
@@ -485,15 +591,16 @@
     blocks = send_faces.shape[0]
     materials = impedance.shape[0]
     devices = lax.axis_size("dom")
+    stages = devices.bit_length() - 1
     f32, i32 = (jnp.float32, jnp.int32)
     vmem = pl.BlockSpec(memory_space=pltpu.VMEM)
     smem = pl.BlockSpec(memory_space=pltpu.SMEM)
-    out, register_out, totals = pl.pallas_call(
+    out, register_out, absorbed = pl.pallas_call(
         functools.partial(step_kernel, devices, face_nodes, rotations),
         out_shape=(
             jax.ShapeDtypeStruct(solution.shape, f32),
             jax.ShapeDtypeStruct(register.shape, f32),
-            jax.ShapeDtypeStruct((2 * materials, LANES), f32),
+            jax.ShapeDtypeStruct((2, materials), f32),
         ),
         in_specs=[vmem] * 5 + [smem] + [vmem] * 8,
         out_specs=(vmem, vmem, vmem),
@@ -515,8 +622,14 @@
             pltpu.VMEM((160, elems), f32),
             pltpu.VMEM((2 * blocks * SLOT, LANES), f32),
             pltpu.VMEM((2 * blocks * SLOT, LANES), f32),
+            pltpu.VMEM((2 * LANES, (rows + blocks) * LANES), jnp.bfloat16),
+            pltpu.VMEM((10 * rows, 2 * LANES), jnp.bfloat16),
+            pltpu.VMEM((stages, 2 * materials, LANES), f32),
+            pltpu.VMEM((stages, 2 * materials, LANES), f32),
             pltpu.SemaphoreType.DMA((2, blocks)),
             pltpu.SemaphoreType.DMA((2, blocks)),
+            pltpu.SemaphoreType.DMA((stages,)),
+            pltpu.SemaphoreType.DMA((stages,)),
         ],
         compiler_params=pltpu.CompilerParams(
             collective_id=0, has_side_effects=True, vmem_limit_bytes=40 * 1024 * 1024
@@ -534,8 +647,6 @@
         send_faces,
         *tables,
     )
-    per_section = jnp.sum(totals, axis=1).reshape(2, materials)
-    absorbed = lax.psum(per_section, "dom") * (NMAT / (devices * elems))
     return (out, register_out, absorbed)
 
 

time: 84.4 us -> 47.4 us (0.56)
  blocking collectives: 41.3 us -> 0 us
  Pallas kernels: 36.3 us -> 40.9 us
    psum x1 -> x0, blocking collectives: 41.3 us -> none  [local(): absorbed = lax.psum(per_section, 'dom') * (NMAT / (devices * elems))]
    pallas_call x1, Pallas kernels: 36.3 us -> 40.9 us  [local(): pl.pallas_call(functools.partial(step_kernel, devices, face_nodes, rotati...]
    pallas_call x0 -> x2, local copies, waits for them, and re-layouts: none -> 2.52 us  [local(): pl.pallas_call(functools.partial(step_kernel, devices, face_nodes, rotati...]
    unnamed x30 -> x29, local copies, waits for them, and re-layouts: 4.94 us -> 2.98 us
where the time goes in v2:
time: 47.4 us; the launch traced here: 47.2 us
  Pallas kernels  40.9 us (86%)
  local copies, waits for them, and re-layouts  5.5 us (12%)
  between operations  0.81 us (2%)
    pallas_call x1, Pallas kernels, local(): pl.pallas_call(functools.partial(step_kernel, devices, face_nodes, rotati...  40.9 us
    unnamed x29, local copies, waits for them, and re-layouts  2.98 us
    pallas_call x2, local copies, waits for them, and re-layouts, local(): pl.pallas_call(functools.partial(step_kernel, devices, face_nodes, rotati...  2.52 us

profile of v2, /device:TPU:0, one launch (start us, length us, event | category | flops | bytes accessed | tf_op | source)
XLA Modules:
  0.0 47.2 jit_solution(9388425724638803239)
XLA Ops:
  0.6 0.0 copy-start.12
  0.6 1.5 %copy.15.sol = f32[4,20,2048]{2,1,0:T(8,128)S(1)} copy(f32[4,20,2048]{2,0,1:T(4,128)} %param.12) | data formatting | bytes 1310720 | tf_op args[0]
  2.2 0.0 copy-done.12
  2.2 0.0 copy-start
  2.2 0.0 copy-start.1
  2.2 0.0 copy-start.2
  2.2 0.0 copy-start.3
  2.2 0.0 copy-start.4
  2.2 0.0 copy-start.5
  2.3 0.0 copy-start.6
  2.3 0.0 copy-start.7
  2.3 0.0 copy-start.8
  2.3 0.0 copy-start.9
  2.3 0.0 copy-start.10
  2.3 0.0 copy-start.11
  2.3 0.4 copy.16.reg
  2.7 0.4 copy-done
  3.1 0.1 copy-done.1
  3.1 0.0 copy-done.2
  3.2 0.0 copy-done.3
  3.2 0.0 copy-done.4
  3.2 0.0 copy-done.5
  3.2 0.0 copy-done.6
  3.2 0.0 copy-done.7
  3.2 0.0 copy-done.8
  3.2 0.0 copy-done.9
  3.2 0.0 copy-done.10
  3.2 0.0 copy-done.11
  3.2 40.9 %shard_map.139 = (f32[4,20,2048]{2,1,0:T(8,128)S(1)}, f32[4,20,2048]{2,1,0:T(8,128)S(1)}, f32[2,16]{1,0:T(2,128)S(1)}) custom-call(f32[4,20,2048]{2,1,0:T(8,128)S(1)} %copy.15.sol, f32[4,20,2048]{2,1,0:T(8,128)S(1)} %copy.16.reg, f32[9,2048]{1,0:T(8,128)S(1)} %copy-done, f32[3,4,2048]{2,1,0:T(4,128)S(1)} %copy-done.1, f32[4,2048]{1,0:T(4,128)S(1)} %copy-done.4, ...), custom_call_target="tpu_custom_call" | custom-call | tf_op jit(solution)/shard_map/pallas_call | solution.py:598
  44.1 1.3 %copy.17 = f32[4,20,2048]{2,0,1:T(4,128)} copy(f32[4,20,2048]{2,1,0:T(8,128)S(1)} %get-tuple-element.3) | data formatting | bytes 1310720 | tf_op jit(solution)/shard_map/pallas_call | solution.py:598
  45.4 1.3 %copy.18 = f32[4,20,2048]{2,0,1:T(4,128)} copy(f32[4,20,2048]{2,1,0:T(8,128)S(1)} %get-tuple-element.4) | data formatting | bytes 1310720 | tf_op jit(solution)/shard_map/pallas_call | solution.py:598
  46.6 0.6 %copy.20 = f32[2,16]{1,0:T(2,128)} copy(f32[2,16]{1,0:T(2,128)S(1)} %get-tuple-element.11) | data formatting | bytes 256
Async XLA Ops:
  0.6 1.5 %copy-start.12 = (f32[4,20,2048]{2,0,1:T(4,128)S(1)}, f32[4,20,2048]{2,0,1:T(4,128)}, u32[]{:S(2)}) copy-start(f32[4,20,2048]{2,0,1:T(4,128)} %param.13) | copy-start | bytes 1966084
  2.2 0.9 %copy-start = (f32[9,2048]{1,0:T(8,128)S(1)}, f32[9,2048]{1,0:T(8,128)}, u32[]{:S(2)}) copy-start(f32[9,2048]{1,0:T(8,128)} %geo.1) | copy-start | bytes 221188
  2.2 0.9 %copy-start.1 = (f32[3,4,2048]{2,1,0:T(4,128)S(1)}, f32[3,4,2048]{2,1,0:T(4,128)}, u32[]{:S(2)}) copy-start(f32[3,4,2048]{2,1,0:T(4,128)} %nrm.1) | copy-start | bytes 294916
  2.2 0.9 %copy-start.2 = (bf16[96,160]{1,0:T(8,128)(2,1)S(1)}, bf16[96,160]{1,0:T(8,128)(2,1)}, u32[]{:S(2)}) copy-start(bf16[96,160]{1,0:T(8,128)(2,1)} %constant.14.lift_low) | copy-start | bytes 92164
  2.2 0.9 %copy-start.3 = (bf16[96,160]{1,0:T(8,128)(2,1)S(1)}, bf16[96,160]{1,0:T(8,128)(2,1)}, u32[]{:S(2)}) copy-start(bf16[96,160]{1,0:T(8,128)(2,1)} %constant.11.lift_high) | copy-start | bytes 92164
  2.2 0.9 %copy-start.4 = (f32[4,2048]{1,0:T(4,128)S(1)}, f32[4,2048]{1,0:T(4,128)}, u32[]{:S(2)}) copy-start(f32[4,2048]{1,0:T(4,128)} %fsc.1) | copy-start | bytes 98308
  2.2 0.9 %copy-start.5 = (s32[4,2048]{1,0:T(4,128)S(1)}, s32[4,2048]{1,0:T(4,128)}, u32[]{:S(2)}) copy-start(s32[4,2048]{1,0:T(4,128)} %nbr.1) | copy-start | bytes 98308
  2.3 0.9 %copy-start.6 = (s32[4,2048]{1,0:T(4,128)S(1)}, s32[4,2048]{1,0:T(4,128)}, u32[]{:S(2)}) copy-start(s32[4,2048]{1,0:T(4,128)} %ori.1) | copy-start | bytes 98308
  2.3 0.9 %copy-start.7 = (s32[4,2048]{1,0:T(4,128)S(1)}, s32[4,2048]{1,0:T(4,128)}, u32[]{:S(2)}) copy-start(s32[4,2048]{1,0:T(4,128)} %mat.1) | copy-start | bytes 98308
  2.3 0.9 %copy-start.8 = (bf16[96,96]{1,0:T(8,128)(2,1)S(1)}, bf16[96,96]{1,0:T(8,128)(2,1)}, u32[]{:S(2)}) copy-start(bf16[96,96]{1,0:T(8,128)(2,1)} %constant.10.vol_low) | copy-start | bytes 55300
  2.3 0.9 %copy-start.9 = (bf16[96,96]{1,0:T(8,128)(2,1)S(1)}, bf16[96,96]{1,0:T(8,128)(2,1)}, u32[]{:S(2)}) copy-start(bf16[96,96]{1,0:T(8,128)(2,1)} %constant.7.vol_high) | copy-start | bytes 55300
  2.3 0.9 %copy-start.10 = (s32[8,128]{1,0:T(8,128)S(1)}, s32[8,128]{1,0:T(8,128)}, u32[]{:S(2)}) copy-start(s32[8,128]{1,0:T(8,128)} %snd.1) | copy-start | bytes 12292
  2.3 0.9 %copy-start.11 = (f32[16]{0:T(128)S(1)}, f32[16]{0:T(128)}, u32[]{:S(2)}) copy-start(f32[16]{0:T(128)} %imp.1) | copy-start | bytes 196

commit v3 on v2

--- a/solution.py
+++ b/solution.py
@@ -156,14 +156,14 @@
     single = jnp.asarray(table, dtype=jnp.float32)
     high = single.astype(jnp.bfloat16)
     low = (single - high.astype(jnp.float32)).astype(jnp.bfloat16)
-    return (high, low)
-
-
-def split_dot(high, low, values):
-    value_high = values.astype(jnp.bfloat16)
-    value_low = (values - value_high.astype(jnp.float32)).astype(jnp.bfloat16)
-    dot = functools.partial(jnp.dot, preferred_element_type=jnp.float32)
-    return dot(high, value_high) + (dot(high, value_low) + dot(low, value_high))
+    return jnp.concatenate([high, high, low], axis=1)
+
+
+def split_dot(parts, values):
+    high = values.astype(jnp.bfloat16)
+    low = (values - high.astype(jnp.float32)).astype(jnp.bfloat16)
+    stacked = jnp.concatenate([high, low, high], axis=0)
+    return jnp.dot(parts, stacked, preferred_element_type=jnp.float32)
 
 
 def lane_pick(row, lanes):
@@ -185,10 +185,8 @@
     ori,
     mat,
     snd,
-    vol_high,
-    vol_low,
-    lift_high,
-    lift_low,
+    vol_parts,
+    lift_parts,
     sol_out,
     reg_out,
     tot_out,
@@ -452,7 +450,7 @@
         if section == 1:
             part_copy(0).start()
 
-        def volume_chunk(c, carry):
+        def volume_chunk(c):
             at = pl.ds(pl.multiple_of(c * CHUNK, CHUNK), CHUNK)
             velocity = [sol_in[i + 1, :, at] for i in range(3)]
             metric = geo[:, at]
@@ -463,7 +461,7 @@
                     + metric[6 + a : 7 + a] * velocity[2]
                 )
             yv[3 * PAD : 3 * PAD + 20, at] = sol_in[0, :, at]
-            out = split_dot(vol_high[...], vol_low[...], yv[:, at])
+            out = split_dot(vol_parts[...], yv[:, at])
             vol[0:PAD, at] = out[0:PAD]
             grads = [out[(a + 1) * PAD : (a + 2) * PAD] for a in range(3)]
             for i in range(3):
@@ -472,11 +470,8 @@
                     + metric[3 * i + 1 : 3 * i + 2] * grads[1]
                     + metric[3 * i + 2 : 3 * i + 3] * grads[2]
                 )
-            return carry
-
-        lax.fori_loop(0, elems // CHUNK, volume_chunk, 0)
-
-        def local_pair(q, carry):
+
+        def matmul_pair(q):
             first = q * 2
             column = pl.multiple_of(first * LANES, 2 * LANES)
             found = pick_tile(column, [code_d[pl.ds(first + h, 1), :] for h in range(2)])
@@ -485,16 +480,39 @@
                 acc[pl.ds(first + h, SUB, stride=rows), :] = main
                 for r in range(2):
                     acc[pl.ds((SUB + r) * rows + first + h, 1), :] = rest[r]
+
+        def pick_rows(at, start, count):
+            at = pl.multiple_of(at, SUB)
+            planes = [pl.ds(pl.multiple_of(n * rows + at, SUB), SUB) for n in range(10)]
+            code = code_d[pl.ds(at, SUB), :]
+            high = (code >> 7) - start
+            low = code & (LANES - 1)
+            values = [acc[plane, :] for plane in planes]
+            for k in range(count):
+                hit = high == k
+                for n in range(10):
+                    row = tab[pl.ds(n * rows + start + k, 1), :]
+                    values[n] = jnp.where(hit, lane_pick(row, low), values[n])
+            for n in range(10):
+                acc[planes[n], :] = values[n]
+
+        def local_step(i, carry):
+            volume_chunk(i)
+            matmul_pair(2 * i)
+            matmul_pair(2 * i + 1)
+            pick_rows(rows // 2 + (i // 2) * SUB, (i % 2) * (rows // 2), rows // 2)
             return carry
 
+        for n in range(10):
+            half = slice(n * rows + rows // 2, (n + 1) * rows)
+            acc[half, :] = jnp.zeros((rows // 2, LANES), jnp.float32)
         if section == 0:
-            lax.fori_loop(0, rows // 2, local_pair, 0)
+            lax.fori_loop(0, groups, local_step, 0)
         else:
+            lax.fori_loop(0, groups // 2, local_step, 0)
             advance(0)
-            lax.fori_loop(0, rows // 4, local_pair, 0)
+            lax.fori_loop(groups // 2, groups, local_step, 0)
             advance(1)
-            lax.fori_loop(rows // 4, rows // 2, local_pair, 0)
-            advance(2)
 
         for j in range(blocks):
 
@@ -532,7 +550,7 @@
 
         lax.fori_loop(0, groups, finish_rows, 0)
         if section == 1:
-            advance(3)
+            advance(2)
 
         for eb in range(eb_count):
             lanes = slice(eb * LANES, (eb + 1) * LANES)
@@ -545,11 +563,11 @@
                     fl[first : first + SUB, lanes] = -normal[i] * flux
 
         if section == 1:
-            advance(4)
+            advance(3)
 
         def update_chunk(c, carry):
             at = pl.ds(pl.multiple_of(c * CHUNK, CHUNK), CHUNK)
-            lifted = split_dot(lift_high[...], lift_low[...], fl[:, at])
+            lifted = split_dot(lift_parts[...], fl[:, at])
             for field in range(4):
                 rhs = lifted[field * PAD : field * PAD + 20] + vol[field * PAD : field * PAD + 20, at]
                 new = section_decay[section] * reg_in[field, :, at] + time_step * rhs
@@ -557,9 +575,9 @@
                 reg_out[field, :, at] = new
             return carry
 
-        lax.fori_loop(0, elems // CHUNK, update_chunk, 0)
-
-    for s in range(5, stages):
+        lax.fori_loop(0, elems // CHUNK, update_chunk, 0, unroll=4)
+
+    for s in range(4, stages):
         advance(s)
     for s in range(stages):
         part_copy(s).wait_send()
@@ -585,7 +603,7 @@
     send_faces,
 ):
     volume, lift, face_nodes, rotations = operator_tables()
-    tables = split_table(volume) + split_table(lift)
+    tables = (split_table(volume), split_table(lift))
     elems = solution.shape[2]
     rows = 4 * elems // LANES
     blocks = send_faces.shape[0]
@@ -602,7 +620,7 @@
             jax.ShapeDtypeStruct(register.shape, f32),
             jax.ShapeDtypeStruct((2, materials), f32),
         ),
-        in_specs=[vmem] * 5 + [smem] + [vmem] * 8,
+        in_specs=[vmem] * 5 + [smem] + [vmem] * 6,
         out_specs=(vmem, vmem, vmem),
         scratch_shapes=[
             pltpu.VMEM((20 * rows, LANES), f32),

time: 47.4 us -> 36.4 us (0.77)
  Pallas kernels: 40.9 us -> 29.8 us
    pallas_call x1, Pallas kernels: 40.9 us -> 29.8 us  [local(): pl.pallas_call(functools.partial(step_kernel, devices, face_nodes, rotati...]
    unnamed x29 -> x25, local copies, waits for them, and re-layouts: 2.98 us -> 3.08 us
where the time goes in v3:
time: 36.4 us; the launch traced here: 36.2 us
  Pallas kernels  29.8 us (82%)
  local copies, waits for them, and re-layouts  5.6 us (15%)
  between operations  0.77 us (2%)
    pallas_call x1, Pallas kernels, local(): pl.pallas_call(functools.partial(step_kernel, devices, face_nodes, rotati...  29.8 us
    unnamed x25, local copies, waits for them, and re-layouts  3.08 us
    pallas_call x2, local copies, waits for them, and re-layouts, local(): pl.pallas_call(functools.partial(step_kernel, devices, face_nodes, rotati...  2.52 us

profile of v3, /device:TPU:0, one launch (start us, length us, event | category | flops | bytes accessed | tf_op | source)
XLA Modules:
  0.0 36.2 jit_solution(14882756814910700983)
XLA Ops:
  0.6 0.0 copy-start.10
  0.6 1.5 %copy.15.sol = f32[4,20,2048]{2,1,0:T(8,128)S(1)} copy(f32[4,20,2048]{2,0,1:T(4,128)} %param.12) | data formatting | bytes 1310720 | tf_op args[0]
  2.2 0.0 copy-done.10
  2.2 0.0 copy-start
  2.2 0.0 copy-start.1
  2.2 0.0 copy-start.2
  2.2 0.0 copy-start.3
  2.2 0.0 copy-start.4
  2.2 0.0 copy-start.5
  2.3 0.0 copy-start.6
  2.3 0.0 copy-start.7
  2.3 0.0 copy-start.8
  2.3 0.0 copy-start.9
  2.3 0.4 %copy.16.reg = f32[4,20,2048]{2,1,0:T(8,128)S(1)} copy(f32[4,20,2048]{2,0,1:T(4,128)S(1)} %copy-done.10) | data formatting | bytes 1310720 | tf_op args[1]
  2.7 0.4 %copy-done = f32[9,2048]{1,0:T(8,128)S(1)} copy-done((f32[9,2048]{1,0:T(8,128)S(1)}, f32[9,2048]{1,0:T(8,128)}, u32[]{:S(2)}) %copy-start) | copy-done | bytes 73752
  3.1 0.1 copy-done.1
  3.1 0.0 copy-done.2
  3.2 0.0 copy-done.3
  3.2 0.0 copy-done.4
  3.2 0.0 copy-done.5
  3.2 0.0 copy-done.6
  3.2 0.0 copy-done.7
  3.3 0.0 copy-done.8
  3.3 0.0 copy-done.9
  3.3 29.8 %shard_map.139 = (f32[4,20,2048]{2,1,0:T(8,128)S(1)}, f32[4,20,2048]{2,1,0:T(8,128)S(1)}, f32[2,16]{1,0:T(2,128)S(1)}) custom-call(f32[4,20,2048]{2,1,0:T(8,128)S(1)} %copy.15.sol, f32[4,20,2048]{2,1,0:T(8,128)S(1)} %copy.16.reg, f32[9,2048]{1,0:T(8,128)S(1)} %copy-done, f32[3,4,2048]{2,1,0:T(4,128)S(1)} %copy-done.1, f32[4,2048]{1,0:T(4,128)S(1)} %copy-done.4, ...), custom_call_target="tpu_custom_call" | custom-call | tf_op jit(solution)/shard_map/pallas_call | solution.py:616
  33.1 1.3 %copy.17 = f32[4,20,2048]{2,0,1:T(4,128)} copy(f32[4,20,2048]{2,1,0:T(8,128)S(1)} %get-tuple-element.3) | data formatting | bytes 1310720 | tf_op jit(solution)/shard_map/pallas_call | solution.py:616
  34.4 1.3 %copy.18 = f32[4,20,2048]{2,0,1:T(4,128)} copy(f32[4,20,2048]{2,1,0:T(8,128)S(1)} %get-tuple-element.4) | data formatting | bytes 1310720 | tf_op jit(solution)/shard_map/pallas_call | solution.py:616
  35.6 0.6 %copy.20 = f32[2,16]{1,0:T(2,128)} copy(f32[2,16]{1,0:T(2,128)S(1)} %get-tuple-element.11) | data formatting | bytes 256
Async XLA Ops:
  0.6 1.5 %copy-start.10 = (f32[4,20,2048]{2,0,1:T(4,128)S(1)}, f32[4,20,2048]{2,0,1:T(4,128)}, u32[]{:S(2)}) copy-start(f32[4,20,2048]{2,0,1:T(4,128)} %param.13) | copy-start | bytes 1966084
  2.2 0.9 %copy-start = (f32[9,2048]{1,0:T(8,128)S(1)}, f32[9,2048]{1,0:T(8,128)}, u32[]{:S(2)}) copy-start(f32[9,2048]{1,0:T(8,128)} %geo.1) | copy-start | bytes 221188
  2.2 0.9 %copy-start.1 = (f32[3,4,2048]{2,1,0:T(4,128)S(1)}, f32[3,4,2048]{2,1,0:T(4,128)}, u32[]{:S(2)}) copy-start(f32[3,4,2048]{2,1,0:T(4,128)} %nrm.1) | copy-start | bytes 294916
  2.2 1.0 %copy-start.2 = (bf16[96,480]{1,0:T(8,128)(2,1)S(1)}, bf16[96,480]{1,0:T(8,128)(2,1)}, u32[]{:S(2)}) copy-start(bf16[96,480]{1,0:T(8,128)(2,1)} %constant.16.lift_parts) | copy-start | bytes 276484
  2.2 1.0 %copy-start.3 = (bf16[96,288]{1,0:T(8,128)(2,1)S(1)}, bf16[96,288]{1,0:T(8,128)(2,1)}, u32[]{:S(2)}) copy-start(bf16[96,288]{1,0:T(8,128)(2,1)} %constant.11.vol_parts) | copy-start | bytes 165892
  2.2 1.0 %copy-start.4 = (f32[4,2048]{1,0:T(4,128)S(1)}, f32[4,2048]{1,0:T(4,128)}, u32[]{:S(2)}) copy-start(f32[4,2048]{1,0:T(4,128)} %fsc.1) | copy-start | bytes 98308
  2.2 1.0 %copy-start.5 = (s32[4,2048]{1,0:T(4,128)S(1)}, s32[4,2048]{1,0:T(4,128)}, u32[]{:S(2)}) copy-start(s32[4,2048]{1,0:T(4,128)} %nbr.1) | copy-start | bytes 98308
  2.3 1.0 %copy-start.6 = (s32[4,2048]{1,0:T(4,128)S(1)}, s32[4,2048]{1,0:T(4,128)}, u32[]{:S(2)}) copy-start(s32[4,2048]{1,0:T(4,128)} %ori.1) | copy-start | bytes 98308
  2.3 1.0 %copy-start.7 = (s32[4,2048]{1,0:T(4,128)S(1)}, s32[4,2048]{1,0:T(4,128)}, u32[]{:S(2)}) copy-start(s32[4,2048]{1,0:T(4,128)} %mat.1) | copy-start | bytes 98308
  2.3 1.0 %copy-start.8 = (s32[8,128]{1,0:T(8,128)S(1)}, s32[8,128]{1,0:T(8,128)}, u32[]{:S(2)}) copy-start(s32[8,128]{1,0:T(8,128)} %snd.1) | copy-start | bytes 12292
  2.3 1.0 %copy-start.9 = (f32[16]{0:T(128)S(1)}, f32[16]{0:T(128)}, u32[]{:S(2)}) copy-start(f32[16]{0:T(128)} %imp.1) | copy-start | bytes 196

commit v4 on v3

--- a/solution.py
+++ b/solution.py
@@ -139,16 +139,18 @@
 def operator_tables():
     grad_rows, lift_rows, face_nodes, rotations = dg_tables()
     grads = np.array(grad_rows, dtype=np.float64).reshape(3, 20, 20)
-    volume = np.zeros((4 * PAD, 4 * PAD))
+    volume = np.zeros((80, 12 * PAD))
     for a in range(3):
-        volume[0:20, a * PAD : a * PAD + 20] = -grads[a]
-        volume[(a + 1) * PAD : (a + 1) * PAD + 20, 3 * PAD : 3 * PAD + 20] = grads[a]
+        volume[0::4, a * PAD : a * PAD + 20] = -grads[a]
+        for i in range(3):
+            first = (3 + 3 * i + a) * PAD
+            volume[i + 1 :: 4, first : first + 20] = -grads[a]
     lift_node_major = np.array(
         [[row[f * 10 + m] for m in range(10) for f in range(4)] for row in lift_rows]
     )
-    lift = np.zeros((4 * PAD, 160))
+    lift = np.zeros((80, 160))
     for field in range(4):
-        lift[field * PAD : field * PAD + 20, field * 40 : field * 40 + 40] = lift_node_major
+        lift[field::4, field * 40 : field * 40 + 40] = lift_node_major
     return (volume, lift, face_nodes, rotations)
 
 
@@ -166,9 +168,8 @@
     return jnp.dot(parts, stacked, preferred_element_type=jnp.float32)
 
 
-def lane_pick(row, lanes):
-    spread = jnp.broadcast_to(row, lanes.shape)
-    return jnp.take_along_axis(spread, lanes, axis=1, mode="promise_in_bounds")
+def lane_pick(source, lanes):
+    return jnp.take_along_axis(source, lanes, axis=1, mode="promise_in_bounds")
 
 
 def step_kernel(
@@ -202,13 +203,15 @@
     half_scale,
     reflect_d,
     loss_d,
-    yv,
+    nat,
     vol,
     fl,
     send_buf,
     recv_buf,
     hot,
     table,
+    spread_tab,
+    spread_recv,
     part_sent,
     part_got,
     send_sem,
@@ -268,9 +271,8 @@
         loss_d[at, :] = jnp.where(code_d[at, :] < 0, loss, 0.0)
         return carry
 
-    lax.fori_loop(0, groups, reflect_rows, 0)
-    for block in range(4):
-        yv[block * PAD + SLOT : (block + 1) * PAD, :] = jnp.zeros((PAD - SLOT, elems), jnp.float32)
+    for field in range(4):
+        nat[field * PAD + SLOT : (field + 1) * PAD, :] = jnp.zeros((PAD - SLOT, elems), jnp.float32)
 
     def copy_out(section, j):
         return pltpu.make_async_remote_copy(
@@ -303,21 +305,48 @@
         hot_rows(code_d[pl.ds(r, 1), :], pl.multiple_of(r * LANES, LANES))
         return carry
 
-    lax.fori_loop(0, rows, hot_face_row, 0)
     for j in range(blocks):
         hot_rows(snd[j : j + 1, :], (rows + j) * LANES)
 
+    half = rows // 2
+
+    def main_at(k):
+        return (k // half) * half * 10 + (k % half) * SUB
+
+    def rest_at(q):
+        return (q // (groups // 2)) * half * 10 + half * SUB + (q % (groups // 2)) * SLOT
+
     def fill_table():
-        for pair in range(rows // 2):
+        for pair in range(half):
             value = jnp.concatenate(
                 [tab[pl.ds(pair * 2 + h, SUB, stride=rows), :] for h in range(2)], axis=0
             )
-            put_split(pair * SLOT, value)
+            put_split(main_at(pair * 2), value)
         for q in range(groups):
             value = jnp.concatenate(
                 [tab[n * rows + q * SUB : n * rows + (q + 1) * SUB, :] for n in (8, 9)], axis=0
             )
-            put_split(rows * SUB + q * SLOT, value)
+            put_split(rest_at(q), value)
+
+    def spread_rows(g, carry):
+        first = pl.multiple_of(g * SUB, SUB)
+        value = tab[pl.ds(first, SUB), :]
+        for r in range(SUB):
+            spot = pl.multiple_of((first + r) * SUB, SUB)
+            spread_tab[pl.ds(spot, SUB), :] = jnp.broadcast_to(value[r : r + 1], (SUB, LANES))
+        return carry
+
+    def pick_some(values, code, start, count):
+        high = (code >> 7) - start
+        low = code & (LANES - 1)
+        values = list(values)
+        for k in range(count):
+            hit = high == k
+            for n in range(10):
+                spot = pl.multiple_of((n * rows + start + k) * SUB, SUB)
+                source = spread_tab[pl.ds(spot, SUB), :]
+                values[n] = jnp.where(hit, lane_pick(source, low), values[n])
+        return values
 
     def put_split(first, value):
         high = value.astype(jnp.bfloat16)
@@ -326,23 +355,25 @@
             value - high.astype(jnp.float32)
         ).astype(jnp.bfloat16)
 
-    def pick_tile(column, codes):
+    def pick_tile(column, codes, halves):
         product = jnp.dot(
-            table[...], hot[:, pl.ds(column, 2 * LANES)], preferred_element_type=jnp.float32
+            table[0 : halves * half * 10, :],
+            hot[:, pl.ds(column, 2 * LANES)],
+            preferred_element_type=jnp.float32,
         )
         found = []
         for h in range(2):
             lanes = slice(h * LANES, (h + 1) * LANES)
             high = jnp.broadcast_to(codes[h] >> 7, (SUB, LANES))
             main = jnp.zeros((SUB, LANES), jnp.float32)
-            for k in range(rows):
-                main = jnp.where(high == k, product[k * SUB : (k + 1) * SUB, lanes], main)
+            for k in range(halves * half):
+                main = jnp.where(high == k, product[main_at(k) : main_at(k) + SUB, lanes], main)
             within = high - lax.broadcasted_iota(jnp.int32, (SUB, LANES), 0)
             rest = [jnp.zeros((SUB, LANES), jnp.float32) for _ in range(2)]
-            for q in range(groups):
+            for q in range(halves * groups // 2):
                 hit = within == q * SUB
                 for r in range(2):
-                    first = rows * SUB + q * SLOT + r * SUB
+                    first = rest_at(q) + r * SUB
                     rest[r] = jnp.where(hit, product[first : first + SUB, lanes], rest[r])
             found.append((main, [jnp.sum(r, axis=0, keepdims=True) for r in rest]))
         return found
@@ -381,21 +412,17 @@
         sol_in = sol if section == 0 else sol_out
         reg_in = reg if section == 0 else reg_out
 
-        for field in range(4):
-            for first in range(0, 20, SUB):
-                count = min(SUB, 20 - first)
-                for eb in range(eb_count):
-                    place = pl.ds((field * 20 + first) * eb_count + eb, count, stride=eb_count)
-                    xd[place, :] = sol_in[
-                        field, first : first + count, eb * LANES : (eb + 1) * LANES
-                    ]
+        for node in range(20):
+            for eb in range(eb_count):
+                place = pl.ds(node * 4 * eb_count + eb, 4, stride=eb_count)
+                xd[place, :] = sol_in[node, :, eb * LANES : (eb + 1) * LANES]
 
         for f in range(4):
             normal = [nd[i * rows + f * eb_count : i * rows + (f + 1) * eb_count, :] for i in range(3)]
             for n in range(10):
                 node = face_nodes[f][n]
                 press, u, v, w = [
-                    xd[(field * 20 + node) * eb_count : (field * 20 + node + 1) * eb_count, :]
+                    xd[(node * 4 + field) * eb_count : (node * 4 + field + 1) * eb_count, :]
                     for field in range(4)
                 ]
                 un = normal[0] * u + normal[1] * v + normal[2] * w
@@ -405,19 +432,21 @@
 
         fill_table()
 
-        def send_pair(q, carry):
-            first = q * 2
-            column = pl.multiple_of((rows + first) * LANES, 2 * LANES)
-            found = pick_tile(column, [snd[pl.ds(first + h, 1), :] for h in range(2)])
+        lax.fori_loop(0, 10 * groups, spread_rows, 0, unroll=4)
+
+        picked = pick_some([jnp.zeros((SUB, LANES), jnp.float32)] * 10, snd[...], half, half)
+        for first in range(0, blocks, 2):
+            column = (rows + first) * LANES
+            found = pick_tile(column, [snd[first + h : first + h + 1, :] for h in range(2)], 1)
             for h in range(2):
-                at = pl.multiple_of((section * blocks + first + h) * SLOT, SLOT)
+                at = (section * blocks + first + h) * SLOT
                 main, rest = found[h]
-                send_buf[pl.ds(at, SUB), :] = main
+                send_buf[at : at + SUB, :] = main
                 for r in range(2):
-                    send_buf[pl.ds(at + SUB + r, 1), :] = rest[r]
-            return carry
-
-        lax.fori_loop(0, blocks // 2, send_pair, 0)
+                    send_buf[at + SUB + r : at + SUB + r + 1, :] = rest[r]
+        for n in range(10):
+            place = pl.ds(section * blocks * SLOT + n, blocks, stride=SLOT)
+            send_buf[place, :] = send_buf[place, :] + picked[n]
 
         if section == 0:
             expected = len(far) + sum(v.astype(jnp.int32) for v in valid)
@@ -427,6 +456,10 @@
             @pl.when(valid[j])
             def _():
                 copy_out(section, j).start()
+
+        if section == 0:
+            lax.fori_loop(0, groups, reflect_rows, 0)
+            lax.fori_loop(0, rows, hot_face_row, 0, unroll=2)
 
         def loss_rows(g, sums):
             at = pl.multiple_of(g * SUB, SUB)
@@ -450,31 +483,26 @@
         if section == 1:
             part_copy(0).start()
 
+        for field in range(4):
+            for first in range(0, 20, SUB):
+                count = min(SUB, 20 - first)
+                for eb in range(eb_count):
+                    place = pl.ds((first * 4 + field) * eb_count + eb, count, stride=4 * eb_count)
+                    spot = field * PAD + first
+                    nat[spot : spot + count, eb * LANES : (eb + 1) * LANES] = xd[place, :]
+
         def volume_chunk(c):
             at = pl.ds(pl.multiple_of(c * CHUNK, CHUNK), CHUNK)
-            velocity = [sol_in[i + 1, :, at] for i in range(3)]
-            metric = geo[:, at]
-            for a in range(3):
-                yv[a * PAD : a * PAD + 20, at] = (
-                    metric[a : a + 1] * velocity[0]
-                    + metric[3 + a : 4 + a] * velocity[1]
-                    + metric[6 + a : 7 + a] * velocity[2]
-                )
-            yv[3 * PAD : 3 * PAD + 20, at] = sol_in[0, :, at]
-            out = split_dot(vol_parts[...], yv[:, at])
-            vol[0:PAD, at] = out[0:PAD]
-            grads = [out[(a + 1) * PAD : (a + 2) * PAD] for a in range(3)]
-            for i in range(3):
-                vol[(i + 1) * PAD : (i + 2) * PAD, at] = -(
-                    metric[3 * i : 3 * i + 1] * grads[0]
-                    + metric[3 * i + 1 : 3 * i + 2] * grads[1]
-                    + metric[3 * i + 2 : 3 * i + 3] * grads[2]
-                )
+            press, u, v, w = [nat[f * PAD : (f + 1) * PAD, at] for f in range(4)]
+            metric = [geo[i : i + 1, at] for i in range(9)]
+            terms = [metric[a] * u + metric[3 + a] * v + metric[6 + a] * w for a in range(3)]
+            terms = terms + [metric[i] * press for i in range(9)]
+            vol[:, at] = split_dot(vol_parts[...], jnp.concatenate(terms, axis=0))
 
         def matmul_pair(q):
             first = q * 2
             column = pl.multiple_of(first * LANES, 2 * LANES)
-            found = pick_tile(column, [code_d[pl.ds(first + h, 1), :] for h in range(2)])
+            found = pick_tile(column, [code_d[pl.ds(first + h, 1), :] for h in range(2)], 2)
             for h in range(2):
                 main, rest = found[h]
                 acc[pl.ds(first + h, SUB, stride=rows), :] = main
@@ -484,15 +512,8 @@
         def pick_rows(at, start, count):
             at = pl.multiple_of(at, SUB)
             planes = [pl.ds(pl.multiple_of(n * rows + at, SUB), SUB) for n in range(10)]
-            code = code_d[pl.ds(at, SUB), :]
-            high = (code >> 7) - start
-            low = code & (LANES - 1)
             values = [acc[plane, :] for plane in planes]
-            for k in range(count):
-                hit = high == k
-                for n in range(10):
-                    row = tab[pl.ds(n * rows + start + k, 1), :]
-                    values[n] = jnp.where(hit, lane_pick(row, low), values[n])
+            values = pick_some(values, code_d[pl.ds(at, SUB), :], start, count)
             for n in range(10):
                 acc[planes[n], :] = values[n]
 
@@ -500,12 +521,11 @@
             volume_chunk(i)
             matmul_pair(2 * i)
             matmul_pair(2 * i + 1)
-            pick_rows(rows // 2 + (i // 2) * SUB, (i % 2) * (rows // 2), rows // 2)
+            pick_rows(half + (i // 2) * SUB, (i % 2) * half, half)
             return carry
 
         for n in range(10):
-            half = slice(n * rows + rows // 2, (n + 1) * rows)
-            acc[half, :] = jnp.zeros((rows // 2, LANES), jnp.float32)
+            acc[n * rows + half : (n + 1) * rows, :] = jnp.zeros((half, LANES), jnp.float32)
         if section == 0:
             lax.fori_loop(0, groups, local_step, 0)
         else:
@@ -519,6 +539,14 @@
             @pl.when(valid[j])
             def _():
                 copy_in(section, j).wait_recv()
+
+        for j in range(blocks):
+            for n in range(10):
+                spot = (section * blocks + j) * SLOT + n
+                to = (j * 10 + n) * SUB
+                spread_recv[to : to + SUB, :] = jnp.broadcast_to(
+                    recv_buf[spot : spot + 1, :], (SUB, LANES)
+                )
 
         def finish_rows(g, carry):
             at = pl.multiple_of(g * SUB, SUB)
@@ -531,9 +559,9 @@
             for j in range(blocks):
                 hit = high == rows + j
                 for n in range(10):
-                    spot = (section * blocks + j) * SLOT + n
-                    row = recv_buf[spot : spot + 1, :]
-                    values[n] = jnp.where(hit, lane_pick(row, low), values[n])
+                    spot = (j * 10 + n) * SUB
+                    source = spread_recv[spot : spot + SUB, :]
+                    values[n] = jnp.where(hit, lane_pick(source, low), values[n])
             turn = orient_d[here, :]
             wall = code < 0
             reflect = reflect_d[here, :]
@@ -567,12 +595,12 @@
 
         def update_chunk(c, carry):
             at = pl.ds(pl.multiple_of(c * CHUNK, CHUNK), CHUNK)
-            lifted = split_dot(lift_parts[...], fl[:, at])
-            for field in range(4):
-                rhs = lifted[field * PAD : field * PAD + 20] + vol[field * PAD : field * PAD + 20, at]
-                new = section_decay[section] * reg_in[field, :, at] + time_step * rhs
-                sol_out[field, :, at] = sol_in[field, :, at] + section_weight[section] * new
-                reg_out[field, :, at] = new
+            rhs = split_dot(lift_parts[...], fl[:, at]) + vol[:, at]
+            for node in range(20):
+                change = time_step * rhs[node * 4 : node * 4 + 4]
+                new = section_decay[section] * reg_in[node, :, at] + change
+                sol_out[node, :, at] = sol_in[node, :, at] + section_weight[section] * new
+                reg_out[node, :, at] = new
             return carry
 
         lax.fori_loop(0, elems // CHUNK, update_chunk, 0, unroll=4)
@@ -616,8 +644,8 @@
     out, register_out, absorbed = pl.pallas_call(
         functools.partial(step_kernel, devices, face_nodes, rotations),
         out_shape=(
-            jax.ShapeDtypeStruct(solution.shape, f32),
-            jax.ShapeDtypeStruct(register.shape, f32),
+            jax.ShapeDtypeStruct((20, 4, elems), f32),
+            jax.ShapeDtypeStruct((20, 4, elems), f32),
             jax.ShapeDtypeStruct((2, materials), f32),
         ),
         in_specs=[vmem] * 5 + [smem] + [vmem] * 6,
@@ -636,12 +664,14 @@
             pltpu.VMEM((rows, LANES), f32),
             pltpu.VMEM((rows, LANES), f32),
             pltpu.VMEM((4 * PAD, elems), f32),
-            pltpu.VMEM((4 * PAD, elems), f32),
+            pltpu.VMEM((80, elems), f32),
             pltpu.VMEM((160, elems), f32),
             pltpu.VMEM((2 * blocks * SLOT, LANES), f32),
             pltpu.VMEM((2 * blocks * SLOT, LANES), f32),
             pltpu.VMEM((2 * LANES, (rows + blocks) * LANES), jnp.bfloat16),
             pltpu.VMEM((10 * rows, 2 * LANES), jnp.bfloat16),
+            pltpu.VMEM((10 * rows * SUB, LANES), f32),
+            pltpu.VMEM((10 * blocks * SUB, LANES), f32),
             pltpu.VMEM((stages, 2 * materials, LANES), f32),
             pltpu.VMEM((stages, 2 * materials, LANES), f32),
             pltpu.SemaphoreType.DMA((2, blocks)),
@@ -653,8 +683,8 @@
             collective_id=0, has_side_effects=True, vmem_limit_bytes=40 * 1024 * 1024
         ),
     )(
-        solution,
-        register,
+        jnp.transpose(solution, (1, 0, 2)),
+        jnp.transpose(register, (1, 0, 2)),
         geometry,
         normals,
         face_scale,
@@ -665,6 +695,8 @@
         send_faces,
         *tables,
     )
+    out = jnp.transpose(out, (1, 0, 2))
+    register_out = jnp.transpose(register_out, (1, 0, 2))
     return (out, register_out, absorbed)
 
 

time: 36.4 us -> 44.3 us (1.22); the launches traced: 36.2 us -> 43.7 us
  local copies, waits for them, and re-layouts: 5.6 us -> 12.4 us
  Pallas kernels: 29.8 us -> 30.6 us
    unnamed x25 -> x27, local copies, waits for them, and re-layouts: 3.08 us -> 12.4 us
    pallas_call x2 -> x0, local copies, waits for them, and re-layouts: 2.52 us -> none  [local(): pl.pallas_call(functools.partial(step_kernel, devices, face_nodes, rotati...]
    pallas_call x1, Pallas kernels: 29.8 us -> 30.6 us  [local(): pl.pallas_call(functools.partial(step_kernel, devices, face_nodes, rotati...]
where the time goes in v4:
time: 44.3 us; the launch traced here: 43.7 us
  Pallas kernels  30.6 us (69%)
  local copies, waits for them, and re-layouts  12.4 us (28%)
  between operations  0.66 us (1%)
    pallas_call x1, Pallas kernels, local(): pl.pallas_call(functools.partial(step_kernel, devices, face_nodes, rotati...  30.6 us
    unnamed x27, local copies, waits for them, and re-layouts  12.4 us

profile of v4, /device:TPU:0, one launch (start us, length us, event | category | flops | bytes accessed | tf_op | source)
XLA Modules:
  0.0 43.7 jit_solution(2547532297084029689)
XLA Ops:
  0.6 0.0 copy-start.11
  0.6 0.6 %copy-done.11 = f32[16]{0:T(128)S(1)} copy-done((f32[16]{0:T(128)S(1)}, f32[16]{0:T(128)}, u32[]{:S(2)}) %copy-start.11) | copy-done | bytes 88
  1.3 0.0 copy-start
  1.3 1.1 %copy-done = f32[4,20,2048]{2,0,1:T(4,128)S(1)} copy-done((f32[4,20,2048]{2,0,1:T(4,128)S(1)}, f32[4,20,2048]{2,0,1:T(4,128)}, u32[]{:S(2)}) %copy-start) | copy-done | bytes 655384
  2.4 0.0 copy-start.1
  2.4 1.1 %copy-done.1 = f32[4,20,2048]{2,0,1:T(4,128)S(1)} copy-done((f32[4,20,2048]{2,0,1:T(4,128)S(1)}, f32[4,20,2048]{2,0,1:T(4,128)}, u32[]{:S(2)}) %copy-start.1) | copy-done | bytes 655384
  3.5 0.0 copy-start.2
  3.5 0.9 %copy-done.2 = bf16[80,864]{1,0:T(8,128)(2,1)S(1)} copy-done((bf16[80,864]{1,0:T(8,128)(2,1)S(1)}, bf16[80,864]{1,0:T(8,128)(2,1)}, u32[]{:S(2)}) %copy-start.2) | copy-done | bytes 138264
  4.4 0.0 copy-start.3
  4.4 0.9 %copy-done.3 = f32[9,2048]{1,0:T(8,128)S(1)} copy-done((f32[9,2048]{1,0:T(8,128)S(1)}, f32[9,2048]{1,0:T(8,128)}, u32[]{:S(2)}) %copy-start.3) | copy-done | bytes 73752
  5.3 0.0 copy-start.4
  5.3 0.9 %copy-done.4 = f32[3,4,2048]{2,1,0:T(4,128)S(1)} copy-done((f32[3,4,2048]{2,1,0:T(4,128)S(1)}, f32[3,4,2048]{2,1,0:T(4,128)}, u32[]{:S(2)}) %copy-start.4) | copy-done | bytes 98328
  6.2 0.0 copy-start.5
  6.2 0.9 %copy-done.5 = bf16[80,480]{1,0:T(8,128)(2,1)S(1)} copy-done((bf16[80,480]{1,0:T(8,128)(2,1)S(1)}, bf16[80,480]{1,0:T(8,128)(2,1)}, u32[]{:S(2)}) %copy-start.5) | copy-done | bytes 76824
  7.1 0.0 copy-start.6
  7.1 0.8 %copy-done.6 = f32[4,2048]{1,0:T(4,128)S(1)} copy-done((f32[4,2048]{1,0:T(4,128)S(1)}, f32[4,2048]{1,0:T(4,128)}, u32[]{:S(2)}) %copy-start.6) | copy-done | bytes 32792
  7.8 0.0 copy-start.7
  7.8 0.8 %copy-done.7 = s32[4,2048]{1,0:T(4,128)S(1)} copy-done((s32[4,2048]{1,0:T(4,128)S(1)}, s32[4,2048]{1,0:T(4,128)}, u32[]{:S(2)}) %copy-start.7) | copy-done | bytes 32792
  8.6 0.0 copy-start.8
  8.6 0.8 %copy-done.8 = s32[4,2048]{1,0:T(4,128)S(1)} copy-done((s32[4,2048]{1,0:T(4,128)S(1)}, s32[4,2048]{1,0:T(4,128)}, u32[]{:S(2)}) %copy-start.8) | copy-done | bytes 32792
  9.3 0.0 copy-start.9
  9.3 0.8 %copy-done.9 = s32[4,2048]{1,0:T(4,128)S(1)} copy-done((s32[4,2048]{1,0:T(4,128)S(1)}, s32[4,2048]{1,0:T(4,128)}, u32[]{:S(2)}) %copy-start.9) | copy-done | bytes 32792
  10.1 0.0 copy-start.10
  10.1 0.7 %copy-done.10 = s32[8,128]{1,0:T(8,128)S(1)} copy-done((s32[8,128]{1,0:T(8,128)S(1)}, s32[8,128]{1,0:T(8,128)}, u32[]{:S(2)}) %copy-start.10) | copy-done | bytes 4120
  10.8 30.6 %shard_map.139 = (f32[20,4,2048]{2,1,0:T(4,128)S(1)}, f32[20,4,2048]{2,1,0:T(4,128)S(1)}, f32[2,16]{1,0:T(2,128)S(1)}) custom-call(f32[20,4,2048]{2,1,0:T(4,128)S(1)} %bitcast.4, f32[20,4,2048]{2,1,0:T(4,128)S(1)} %bitcast.5, f32[9,2048]{1,0:T(8,128)S(1)} %copy-done.3, f32[3,4,2048]{2,1,0:T(4,128)S(1)} %copy-done.4, f32[4,2048]{1,0:T(4,128)S(1)} %copy-done.6, ...), custom_call_target="tpu_custom_call" | custom-call | tf_op jit(solution)/shard_map/pallas_call | solution.py:644
  41.4 0.8 %copy.18 = f32[4,20,2048]{2,0,1:T(4,128)} copy(f32[4,20,2048]{2,0,1:T(4,128)S(1)} %bitcast.7) | data formatting | bytes 1310720
  42.3 0.8 %copy.19 = f32[4,20,2048]{2,0,1:T(4,128)} copy(f32[4,20,2048]{2,0,1:T(4,128)S(1)} %bitcast.6) | data formatting | bytes 1310720
  43.1 0.6 %copy.20 = f32[2,16]{1,0:T(2,128)} copy(f32[2,16]{1,0:T(2,128)S(1)} %get-tuple-element.14) | data formatting | bytes 256
Async XLA Ops:
  0.6 0.7 %copy-start.11 = (f32[16]{0:T(128)S(1)}, f32[16]{0:T(128)}, u32[]{:S(2)}) copy-start(f32[16]{0:T(128)} %imp.1) | copy-start | bytes 196
  1.3 1.1 %copy-start = (f32[4,20,2048]{2,0,1:T(4,128)S(1)}, f32[4,20,2048]{2,0,1:T(4,128)}, u32[]{:S(2)}) copy-start(f32[4,20,2048]{2,0,1:T(4,128)} %param.12) | copy-start | bytes 1966084
  2.4 1.1 %copy-start.1 = (f32[4,20,2048]{2,0,1:T(4,128)S(1)}, f32[4,20,2048]{2,0,1:T(4,128)}, u32[]{:S(2)}) copy-start(f32[4,20,2048]{2,0,1:T(4,128)} %param.13) | copy-start | bytes 1966084
  3.5 0.9 %copy-start.2 = (bf16[80,864]{1,0:T(8,128)(2,1)S(1)}, bf16[80,864]{1,0:T(8,128)(2,1)}, u32[]{:S(2)}) copy-start(bf16[80,864]{1,0:T(8,128)(2,1)} %constant.11.vol_parts) | copy-start | bytes 414724
  4.4 0.9 %copy-start.3 = (f32[9,2048]{1,0:T(8,128)S(1)}, f32[9,2048]{1,0:T(8,128)}, u32[]{:S(2)}) copy-start(f32[9,2048]{1,0:T(8,128)} %geo.1) | copy-start | bytes 221188
  5.3 0.9 %copy-start.4 = (f32[3,4,2048]{2,1,0:T(4,128)S(1)}, f32[3,4,2048]{2,1,0:T(4,128)}, u32[]{:S(2)}) copy-start(f32[3,4,2048]{2,1,0:T(4,128)} %nrm.1) | copy-start | bytes 294916
  6.2 0.9 %copy-start.5 = (bf16[80,480]{1,0:T(8,128)(2,1)S(1)}, bf16[80,480]{1,0:T(8,128)(2,1)}, u32[]{:S(2)}) copy-start(bf16[80,480]{1,0:T(8,128)(2,1)} %constant.16.lift_parts) | copy-start | bytes 230404
  7.1 0.8 %copy-start.6 = (f32[4,2048]{1,0:T(4,128)S(1)}, f32[4,2048]{1,0:T(4,128)}, u32[]{:S(2)}) copy-start(f32[4,2048]{1,0:T(4,128)} %fsc.1) | copy-start | bytes 98308
  7.8 0.8 %copy-start.7 = (s32[4,2048]{1,0:T(4,128)S(1)}, s32[4,2048]{1,0:T(4,128)}, u32[]{:S(2)}) copy-start(s32[4,2048]{1,0:T(4,128)} %nbr.1) | copy-start | bytes 98308
  8.6 0.8 %copy-start.8 = (s32[4,2048]{1,0:T(4,128)S(1)}, s32[4,2048]{1,0:T(4,128)}, u32[]{:S(2)}) copy-start(s32[4,2048]{1,0:T(4,128)} %ori.1) | copy-start | bytes 98308
  9.3 0.8 %copy-start.9 = (s32[4,2048]{1,0:T(4,128)S(1)}, s32[4,2048]{1,0:T(4,128)}, u32[]{:S(2)}) copy-start(s32[4,2048]{1,0:T(4,128)} %mat.1) | copy-start | bytes 98308
  10.1 0.7 %copy-start.10 = (s32[8,128]{1,0:T(8,128)S(1)}, s32[8,128]{1,0:T(8,128)}, u32[]{:S(2)}) copy-start(s32[8,128]{1,0:T(8,128)} %snd.1) | copy-start | bytes 12292

commit v5 on v4

--- a/solution.py
+++ b/solution.py
@@ -168,7 +168,8 @@
     return jnp.dot(parts, stacked, preferred_element_type=jnp.float32)
 
 
-def lane_pick(source, lanes):
+def lane_pick(row, lanes):
+    source = jnp.broadcast_to(row, lanes.shape)
     return jnp.take_along_axis(source, lanes, axis=1, mode="promise_in_bounds")
 
 
@@ -176,49 +177,48 @@
     devices,
     face_nodes,
     rotations,
-    sol,
-    reg,
-    geo,
-    nrm,
-    fsc,
-    imp,
-    nbr,
-    ori,
-    mat,
-    snd,
-    vol_parts,
-    lift_parts,
-    sol_out,
-    reg_out,
-    tot_out,
-    xd,
-    tab,
-    hd,
-    acc,
-    nd,
-    n2,
-    code_d,
-    orient_d,
-    mat_d,
-    half_scale,
-    reflect_d,
-    loss_d,
-    nat,
-    vol,
-    fl,
-    send_buf,
-    recv_buf,
-    hot,
-    table,
-    spread_tab,
-    spread_recv,
-    part_sent,
-    part_got,
-    send_sem,
-    recv_sem,
-    part_send_sem,
-    part_recv_sem,
+    *refs,
 ):
+    inputs = refs[:12]
+    (
+        sol_out,
+        reg_out,
+        tot_out,
+        xd,
+        tab,
+        hd,
+        acc,
+        nd,
+        n2,
+        code_d,
+        orient_d,
+        mat_d,
+        half_scale,
+        reflect_d,
+        loss_d,
+        nat,
+        vol,
+        fl,
+        send_buf,
+        recv_buf,
+        hot,
+        table,
+        part_sent,
+        part_got,
+        send_sem,
+        recv_sem,
+        part_send_sem,
+        part_recv_sem,
+        in_sem,
+        *held,
+    ) = refs[12:]
+    loads = [
+        pltpu.make_async_copy(source, target, in_sem.at[i])
+        for i, (source, target) in enumerate(zip(inputs, held))
+    ]
+    for i in (0, 3, 9, 2, 4, 5, 6, 7, 8, 10, 11, 1):
+        loads[i].start()
+    sol, reg, geo, nrm, fsc, imp, nbr, ori, mat, snd, vol_parts, lift_parts = held
     elems = sol.shape[2]
     eb_count = elems // LANES
     rows = 4 * eb_count
@@ -246,18 +246,25 @@
     for s in far:
         pl.semaphore_signal(barrier, inc=1, device_id=(partners[s],), device_id_type=MESH)
 
-    for i in range(3):
-        n2[i, 0:4, :] = nrm[i]
-        n2[i, 4:8, :] = nrm[i]
+    loads[3].wait()
     for eb in range(eb_count):
         lanes = slice(eb * LANES, (eb + 1) * LANES)
-        spread = pl.ds(eb, 4, stride=eb_count)
         for i in range(3):
             nd[pl.ds(i * rows + eb, 4, stride=eb_count), :] = nrm[i, :, lanes]
-        half_scale[spread, :] = 0.5 * fsc[:, lanes]
-        code_d[spread, :] = nbr[:, lanes]
-        orient_d[spread, :] = ori[:, lanes]
-        mat_d[spread, :] = mat[:, lanes]
+
+    def face_tables():
+        for i in (4, 5, 6, 7, 8):
+            loads[i].wait()
+        for i in range(3):
+            n2[i, 0:4, :] = nrm[i]
+            n2[i, 4:8, :] = nrm[i]
+        for eb in range(eb_count):
+            lanes = slice(eb * LANES, (eb + 1) * LANES)
+            spread = pl.ds(eb, 4, stride=eb_count)
+            half_scale[spread, :] = 0.5 * fsc[:, lanes]
+            code_d[spread, :] = nbr[:, lanes]
+            orient_d[spread, :] = ori[:, lanes]
+            mat_d[spread, :] = mat[:, lanes]
 
     def reflect_rows(g, carry):
         at = pl.ds(pl.multiple_of(g * SUB, SUB), SUB)
@@ -305,8 +312,10 @@
         hot_rows(code_d[pl.ds(r, 1), :], pl.multiple_of(r * LANES, LANES))
         return carry
 
+    loads[9].wait()
     for j in range(blocks):
         hot_rows(snd[j : j + 1, :], (rows + j) * LANES)
+    loads[0].wait()
 
     half = rows // 2
 
@@ -328,14 +337,6 @@
             )
             put_split(rest_at(q), value)
 
-    def spread_rows(g, carry):
-        first = pl.multiple_of(g * SUB, SUB)
-        value = tab[pl.ds(first, SUB), :]
-        for r in range(SUB):
-            spot = pl.multiple_of((first + r) * SUB, SUB)
-            spread_tab[pl.ds(spot, SUB), :] = jnp.broadcast_to(value[r : r + 1], (SUB, LANES))
-        return carry
-
     def pick_some(values, code, start, count):
         high = (code >> 7) - start
         low = code & (LANES - 1)
@@ -343,9 +344,8 @@
         for k in range(count):
             hit = high == k
             for n in range(10):
-                spot = pl.multiple_of((n * rows + start + k) * SUB, SUB)
-                source = spread_tab[pl.ds(spot, SUB), :]
-                values[n] = jnp.where(hit, lane_pick(source, low), values[n])
+                row = tab[pl.ds(n * rows + start + k, 1), :]
+                values[n] = jnp.where(hit, lane_pick(row, low), values[n])
         return values
 
     def put_split(first, value):
@@ -432,8 +432,6 @@
 
         fill_table()
 
-        lax.fori_loop(0, 10 * groups, spread_rows, 0, unroll=4)
-
         picked = pick_some([jnp.zeros((SUB, LANES), jnp.float32)] * 10, snd[...], half, half)
         for first in range(0, blocks, 2):
             column = (rows + first) * LANES
@@ -458,6 +456,7 @@
                 copy_out(section, j).start()
 
         if section == 0:
+            face_tables()
             lax.fori_loop(0, groups, reflect_rows, 0)
             lax.fori_loop(0, rows, hot_face_row, 0, unroll=2)
 
@@ -491,6 +490,10 @@
                     spot = field * PAD + first
                     nat[spot : spot + count, eb * LANES : (eb + 1) * LANES] = xd[place, :]
 
+        if section == 0:
+            loads[2].wait()
+            loads[10].wait()
+
         def volume_chunk(c):
             at = pl.ds(pl.multiple_of(c * CHUNK, CHUNK), CHUNK)
             press, u, v, w = [nat[f * PAD : (f + 1) * PAD, at] for f in range(4)]
@@ -539,14 +542,6 @@
             @pl.when(valid[j])
             def _():
                 copy_in(section, j).wait_recv()
-
-        for j in range(blocks):
-            for n in range(10):
-                spot = (section * blocks + j) * SLOT + n
-                to = (j * 10 + n) * SUB
-                spread_recv[to : to + SUB, :] = jnp.broadcast_to(
-                    recv_buf[spot : spot + 1, :], (SUB, LANES)
-                )
 
         def finish_rows(g, carry):
             at = pl.multiple_of(g * SUB, SUB)
@@ -559,9 +554,9 @@
             for j in range(blocks):
                 hit = high == rows + j
                 for n in range(10):
-                    spot = (j * 10 + n) * SUB
-                    source = spread_recv[spot : spot + SUB, :]
-                    values[n] = jnp.where(hit, lane_pick(source, low), values[n])
+                    spot = (section * blocks + j) * SLOT + n
+                    row = recv_buf[spot : spot + 1, :]
+                    values[n] = jnp.where(hit, lane_pick(row, low), values[n])
             turn = orient_d[here, :]
             wall = code < 0
             reflect = reflect_d[here, :]
@@ -592,6 +587,10 @@
 
         if section == 1:
             advance(3)
+
+        if section == 0:
+            loads[11].wait()
+            loads[1].wait()
 
         def update_chunk(c, carry):
             at = pl.ds(pl.multiple_of(c * CHUNK, CHUNK), CHUNK)
@@ -640,7 +639,23 @@
     stages = devices.bit_length() - 1
     f32, i32 = (jnp.float32, jnp.int32)
     vmem = pl.BlockSpec(memory_space=pltpu.VMEM)
-    smem = pl.BlockSpec(memory_space=pltpu.SMEM)
+    arguments = (
+        jnp.transpose(solution, (1, 0, 2)),
+        jnp.transpose(register, (1, 0, 2)),
+        geometry,
+        normals,
+        face_scale,
+        impedance,
+        neighbour,
+        orientation,
+        wall_material,
+        send_faces,
+        *tables,
+    )
+    held = [
+        (pltpu.SMEM if a is impedance else pltpu.VMEM)(a.shape, a.dtype) for a in arguments
+    ]
+    hbm = pl.BlockSpec(memory_space=pltpu.HBM)
     out, register_out, absorbed = pl.pallas_call(
         functools.partial(step_kernel, devices, face_nodes, rotations),
         out_shape=(
@@ -648,7 +663,7 @@
             jax.ShapeDtypeStruct((20, 4, elems), f32),
             jax.ShapeDtypeStruct((2, materials), f32),
         ),
-        in_specs=[vmem] * 5 + [smem] + [vmem] * 6,
+        in_specs=[hbm] * 12,
         out_specs=(vmem, vmem, vmem),
         scratch_shapes=[
             pltpu.VMEM((20 * rows, LANES), f32),
@@ -670,31 +685,19 @@
             pltpu.VMEM((2 * blocks * SLOT, LANES), f32),
             pltpu.VMEM((2 * LANES, (rows + blocks) * LANES), jnp.bfloat16),
             pltpu.VMEM((10 * rows, 2 * LANES), jnp.bfloat16),
-            pltpu.VMEM((10 * rows * SUB, LANES), f32),
-            pltpu.VMEM((10 * blocks * SUB, LANES), f32),
             pltpu.VMEM((stages, 2 * materials, LANES), f32),
             pltpu.VMEM((stages, 2 * materials, LANES), f32),
             pltpu.SemaphoreType.DMA((2, blocks)),
             pltpu.SemaphoreType.DMA((2, blocks)),
             pltpu.SemaphoreType.DMA((stages,)),
             pltpu.SemaphoreType.DMA((stages,)),
+            pltpu.SemaphoreType.DMA((12,)),
+            *held,
         ],
         compiler_params=pltpu.CompilerParams(
-            collective_id=0, has_side_effects=True, vmem_limit_bytes=40 * 1024 * 1024
+            collective_id=0, has_side_effects=True, vmem_limit_bytes=63 * 1024 * 1024
         ),
-    )(
-        jnp.transpose(solution, (1, 0, 2)),
-        jnp.transpose(register, (1, 0, 2)),
-        geometry,
-        normals,
-        face_scale,
-        impedance,
-        neighbour,
-        orientation,
-        wall_material,
-        send_faces,
-        *tables,
-    )
+    )(*arguments)
     out = jnp.transpose(out, (1, 0, 2))
     register_out = jnp.transpose(register_out, (1, 0, 2))
     return (out, register_out, absorbed)

time: 44.3 us -> 35.8 us (0.81); the launches traced: 43.7 us -> 35.7 us
  local copies, waits for them, and re-layouts: 12.4 us -> 3.46 us
  Pallas kernels: 30.6 us -> 31.5 us
    unnamed x27 -> x7, local copies, waits for them, and re-layouts: 12.4 us -> 3.46 us
    pallas_call x1, Pallas kernels: 30.6 us -> 31.5 us  [local(): pl.pallas_call(functools.partial(step_kernel, devices, face_nodes, rotati...]
where the time goes in v5:
time: 35.8 us; the launch traced here: 35.7 us
  Pallas kernels  31.5 us (88%)
  local copies, waits for them, and re-layouts  3.46 us (10%)
  between operations  0.65 us (2%)
    pallas_call x1, Pallas kernels, local(): pl.pallas_call(functools.partial(step_kernel, devices, face_nodes, rotati...  31.5 us
    unnamed x7, local copies, waits for them, and re-layouts  3.46 us

profile of v5, /device:TPU:0, one launch (start us, length us, event | category | flops | bytes accessed | tf_op | source)
XLA Modules:
  0.0 35.7 jit_solution(2667064540456667039)
XLA Ops:
  0.6 31.5 %shard_map.139 = (f32[20,4,2048]{2,1,0:T(4,128)}, f32[20,4,2048]{2,1,0:T(4,128)}, f32[2,16]{1,0:T(2,128)}) custom-call(f32[20,4,2048]{2,1,0:T(4,128)} %bitcast.4, f32[20,4,2048]{2,1,0:T(4,128)} %bitcast.5, f32[9,2048]{1,0:T(8,128)} %refs_2_.1, f32[3,4,2048]{2,1,0:T(4,128)} %refs_3_.1, f32[4,2048]{1,0:T(4,128)} %refs_4_.1, f32[16]{0:T(128)} %refs_5_.1, ...), custom_call_target="tpu_custom_call" | custom-call | tf_op jit(solution)/shard_map/pallas_call | solution.py:659
  32.2 0.0 copy-start
  32.2 2.0 %copy.18 = f32[4,20,2048]{2,0,1:T(4,128)} copy(f32[4,20,2048]{2,0,1:T(4,128)} %bitcast.7) | data formatting | bytes 1310720
  34.2 0.0 copy-done
  34.2 0.0 copy-start.1
  34.3 0.8 %copy.19 = f32[4,20,2048]{2,0,1:T(4,128)} copy(f32[4,20,2048]{2,0,1:T(4,128)S(1)} %bitcast.6) | data formatting | bytes 1310720
  35.1 0.0 copy-done.1
  35.1 0.6 %copy.20 = f32[2,16]{1,0:T(2,128)} copy(f32[2,16]{1,0:T(2,128)S(1)} %copy-done.1) | data formatting | bytes 256
Async XLA Ops:
  32.2 2.1 %copy-start = (f32[20,4,2048]{2,1,0:T(4,128)S(1)}, f32[20,4,2048]{2,1,0:T(4,128)}, u32[]{:S(2)}) copy-start(f32[20,4,2048]{2,1,0:T(4,128)} %get-tuple-element.7) | copy-start | bytes 1966084
  34.2 0.8 %copy-start.1 = (f32[2,16]{1,0:T(2,128)S(1)}, f32[2,16]{1,0:T(2,128)}, u32[]{:S(2)}) copy-start(f32[2,16]{1,0:T(2,128)} %get-tuple-element.14) | copy-start | bytes 388
